TPU v7x, 512 devices: a whole 4x8x8 slice. The times are simulated.
512 devices in a mesh: dp: 128 (over y, z, core), fsdp: 4 (over x).
Axes of the slice: x: 4, y: 8, z: 8, core: 2. Of those that a mesh axis runs over, the one named last changes fastest.
Arguments:
- inputs: bfloat16 [49152, 2560], P('dp', 'fsdp'), may hold values from -6 to 6
- out_grad: bfloat16 [49152, 2560], P('dp', 'fsdp'), may hold values from -0.0625 to 0.0625
- basis: bfloat16 [2560, 512], P('fsdp'), may hold values from -0.25 to 0.25
- moment_first: float32 [512, 2560], P('dp', 'fsdp'), may hold values from -1.5 to 1.5
- moment_second: float32 [512, 2560], P('dp', 'fsdp'), may hold values from 0.0002 to 0.004
Outputs:
- update: bfloat16 [2560, 2560], P('fsdp')
- new_first: float32 [512, 2560], P('dp', 'fsdp')
- new_second: float32 [512, 2560], P('dp', 'fsdp')
All inputs are finite; a program needn't handle non-finite values.
Results may differ from a plain program's by a relative error of at most 0.0063.
Values may be sent and summed in bfloat16 or wider, within the bound.
No kernel may reach another device: no remote copies, remote signals or barrier semaphores. Data moves between devices by JAX's collectives and lax.ppermute only.
A program may use at most 64 MiB of HBM per device.

v0:
```python
import jax
import jax.numpy as jnp
from jax import lax
from jax.sharding import PartitionSpec as P

STEP = 10


def per_device(inputs, out_grad, basis, moment_first, moment_second):
    partial_proj = jnp.dot(inputs, basis, preferred_element_type=jnp.float32)
    projected = lax.psum(partial_proj, "fsdp")
    projected_in = projected.astype(jnp.bfloat16)
    grad_shard = lax.psum_scatter(
        lax.dot_general(
            projected_in, out_grad, (((0,), (0,)), ((), ())), preferred_element_type=jnp.float32
        ),
        "dp",
        scatter_dimension=0,
        tiled=True,
    )
    new_first = 0.9 * moment_first + 0.1 * grad_shard
    new_second = 0.999 * moment_second + 0.001 * grad_shard * grad_shard
    corrected = new_first / (1.0 - 0.9**STEP)
    scaled = jnp.sqrt(new_second / (1.0 - 0.999**STEP)) + 1e-08
    direction = (corrected / scaled).astype(jnp.bfloat16)
    wide_rows = lax.all_gather(direction, "fsdp", axis=1, tiled=True)
    all_rows = lax.all_gather(wide_rows, "dp", axis=0, tiled=True)
    expanded = jnp.dot(basis, all_rows, preferred_element_type=jnp.float32)
    return (expanded.astype(jnp.bfloat16), new_first, new_second)


def solution(mesh):
    return jax.shard_map(
        per_device,
        mesh=mesh,
        in_specs=(
            P("dp", "fsdp"),
            P("dp", "fsdp"),
            P("fsdp", None),
            P("dp", "fsdp"),
            P("dp", "fsdp"),
        ),
        out_specs=(P("fsdp", None), P("dp", "fsdp"), P("dp", "fsdp")),
        check_vma=False,
    )
```

profile of v0, /device:TPU:1, one launch (start us, length us, event | category | flops | bytes accessed | tf_op | source)
XLA Modules:
  0.0 354.7 jit_solution(9478068774207994738)
XLA Ops:
  7.2 0.0 copy-start
  7.2 0.0 copy-start.1
  7.2 0.0 all-reduce.4.cloned.1.call-start
  7.2 1.0 copy-done
  8.3 1.5 fusion.6
  9.8 0.0 copy-start.2
  9.8 0.0 copy-start.3
  9.8 21.1 %all-reduce.5 = bf16[384,512]{1,0:T(8,128)(2,1)S(1)} all-reduce(f32[384,512]{1,0:T(8,128)S(1)} %fusion.6), channel_id=1, replica_groups=mesh['dp'=128,'fsdp'=4] {'fsdp'}, use_global_device_ids=true, to_apply=%region_0.0 | all-reduce | flops 196608 | bytes 1179648 | tf_op jit(solution)/shard_map/psum | solution.py:11
  30.9 0.0 copy-done.1
  30.9 1.6 fusion.7
  32.6 0.0 all-reduce.4.cloned.1.call-update
  32.6 0.0 all-gather.3.cloned.1.call-start
  32.6 1.3 dynamic-slice
  34.6 204.0 %all-reduce.4.cloned.1.call-done = f32[512,640]{1,0:T(8,128)} async-done(((f32[512,640]{1,0:T(8,128)}), f32[512,640]{1,0:T(8,128)}) %all-reduce.4.cloned.1.call-update) | async-done | bytes 1310736
  238.6 0.0 copy-done.2
  238.6 0.0 copy-done.3
  238.6 1.3 fusion.4
  239.9 9.9 %all_gather.6 = bf16[4,2560]{1,0:T(4,128)(2,1)} all-gather(bf16[4,640]{1,0:T(4,128)(2,1)S(1)} %get-tuple-element.9), channel_id=1, replica_groups=mesh['dp'=128,'fsdp'=4] {'fsdp'}, dimensions={1}, use_global_device_ids=true | all-gather | bytes 25600 | tf_op jit(solution)/shard_map/all_gather | solution.py:26
  249.8 0.0 all-gather.3.cloned.1.call-update
  249.9 84.2 %all-gather.3.cloned.1.call-done = bf16[128,4,2560]{2,1,0:T(4,128)(2,1)} async-done(((bf16[1,4,2560]{2,1,0:T(4,128)(2,1)}), bf16[128,4,2560]{2,1,0:T(4,128)(2,1)}) %all-gather.3.cloned.1.call-update) | async-done | bytes 2621456 | tf_op jit(solution)/shard_map/all_gather | solution.py:27
  334.1 4.1 %reshape.7 = bf16[512,2560]{1,0:T(8,128)(2,1)S(1)} reshape(bf16[128,4,2560]{2,1,0:T(4,128)(2,1)} %all-gather.3.cloned.1.call-done) | data formatting | bytes 5242880
  338.2 3.9 %fusion = bf16[640,2560]{0,1:T(8,128)(2,1)} fusion(bf16[512,2560]{1,0:T(8,128)(2,1)S(1)} %reshape.7, bf16[640,512]{1,0:T(8,128)(2,1)S(1)} %copy-done), kind=kOutput, calls=%fused_computation.1 | convolution fusion | flops 1679360000 | bytes 6553600 | tf_op jit(solution)/shard_map/dot_general | solution.py:28
  342.2 5.7 %copy.9 = bf16[640,2560]{1,0:T(8,128)(2,1)} copy(bf16[640,2560]{0,1:T(8,128)(2,1)} %fusion) | data formatting | bytes 6553600
Async XLA Ops:
  7.2 1.1 copy-start
  7.2 23.7 %copy-start.1 = (bf16[384,640]{1,0:T(8,128)(2,1)S(1)}, bf16[384,640]{1,0:T(8,128)(2,1)}, u32[]{:S(2)}) copy-start(bf16[384,640]{1,0:T(8,128)(2,1)} %param.6) | copy-start | bytes 1474564
  7.2 231.4 %all-reduce.4.cloned.1.call-start = ((), (), s32[]{:S(2)}) async-start(), calls=%async_computation.1 | async-start | bytes 2621440
  9.8 228.8 %copy-start.2 = (f32[4,640]{1,0:T(4,128)S(1)}, f32[4,640]{1,0:T(4,128)}, u32[]{:S(2)}) copy-start(f32[4,640]{1,0:T(4,128)} %param.8) | copy-start | bytes 30724
  9.8 228.8 %copy-start.3 = (f32[4,640]{1,0:T(4,128)S(1)}, f32[4,640]{1,0:T(4,128)}, u32[]{:S(2)}) copy-start(f32[4,640]{1,0:T(4,128)} %param.9) | copy-start | bytes 30724
  32.6 301.5 %all-gather.3.cloned.1.call-start = ((), (), s32[]{:S(2)}) async-start(), calls=%async_computation | async-start | bytes 2641920 | tf_op jit(solution)/shard_map/all_gather | solution.py:27
Sparse Core Ops, SparseCore 0:
  32.7 205.7 all-reduce.3
  250.0 84.0 all-gather.2
where the time goes:
time: 355 us
  waiting for transfers between devices  288 us (81%)
  blocking collectives  31.1 us (9%)
  between operations  14.8 us (4%)
  local copies, waits for them, and re-layouts  12.1 us (3%)
  matrix products  7.05 us (2%)
    unnamed x3, waiting for transfers between devices  204 us
    all_gather x1, waiting for transfers between devices, per_device(): all_rows = lax.all_gather(wide_rows, 'dp', axis=0, tiled=True)  84.2 us
    psum x1, blocking collectives, per_device(): projected = lax.psum(partial_proj, 'fsdp')  21.1 us
    unnamed x11, local copies, waits for them, and re-layouts  12.1 us
    all_gather x1, blocking collectives, per_device(): wide_rows = lax.all_gather(direction, 'fsdp', axis=1, tiled=True)  9.94 us
  transfers between devices with their start and end apart: 2, of which 2 were waited for; matrix products, arithmetic and copies ran while one was open for 0% of the time, Pallas kernels for 0%

commit v1 on v0

v1 whole, which is shorter than its diff:
```python
import jax
import jax.numpy as jnp
from jax import lax
from jax.sharding import Mesh, PartitionSpec as P

STEP = 10
F32 = jnp.float32
BF16 = jnp.bfloat16


def spread(block, axes, n):
    return lax.all_to_all(jnp.broadcast_to(block[None], (n,) + block.shape), axes, 0, 0)


def per_device(ny, nz, nx, inputs, out_grad, basis, moment_first, moment_second):
    rank = basis.shape[1]
    groups = ny * nz
    own = moment_first.shape[0]
    half = rank // 2
    core = lax.axis_index("c")

    old = lax.broadcasted_iota(jnp.int32, (rank, rank), 0)
    new = lax.broadcasted_iota(jnp.int32, (rank, rank), 1)
    side = (new // half + core) % 2
    wanted = (new % half) // own * (2 * own) + side * own + new % own
    basis = jnp.dot(basis, (old == wanted).astype(BF16), preferred_element_type=F32).astype(BF16)

    partial = jnp.dot(inputs, basis, preferred_element_type=F32).astype(BF16)
    parts = spread(partial, "x", nx)
    projected = jnp.sum(parts.astype(F32), axis=0).astype(BF16)
    grad = lax.dot_general(projected, out_grad, (((0,), (0,)), ((), ())), preferred_element_type=F32)

    swap = [(0, 1), (1, 0)]
    theirs = lax.ppermute(grad[half:], "c", swap)
    chip = (grad[:half] + theirs).astype(BF16).reshape(groups, own, -1)
    grad_shard = jnp.sum(lax.all_to_all(chip, ("y", "z"), 0, 0).astype(F32), axis=0)

    new_first = 0.9 * moment_first + 0.1 * grad_shard
    new_second = 0.999 * moment_second + 0.001 * grad_shard * grad_shard
    corrected = new_first / (1.0 - 0.9**STEP)
    scaled = jnp.sqrt(new_second / (1.0 - 0.999**STEP)) + 1e-08
    direction = (corrected / scaled).astype(BF16)

    rows = spread(direction, ("y", "z"), groups).reshape(half, -1)
    mine = spread(rows, "x", nx)
    other = lax.ppermute(mine, "c", swap)
    update = [
        (
            jnp.dot(basis[:, :half], mine[i], preferred_element_type=F32)
            + jnp.dot(basis[:, half:], other[i], preferred_element_type=F32)
        ).astype(BF16)
        for i in range(nx)
    ]
    return (jnp.concatenate(update, axis=1), new_first, new_second)


def solution(mesh):
    ny, nz, nx = 8, 8, mesh.devices.shape[1]
    split = Mesh(mesh.devices.reshape(ny, nz, 2, nx), ("y", "z", "c", "x"))
    dp = ("y", "z", "c")

    def body(*args):
        return per_device(ny, nz, nx, *args)

    return jax.shard_map(
        body,
        mesh=split,
        in_specs=(P(dp, "x"), P(dp, "x"), P("x", None), P(dp, "x"), P(dp, "x")),
        out_specs=(P("x", None), P(dp, "x"), P(dp, "x")),
        check_vma=False,
    )
```

time: 355 us -> 129 us (0.36)
  waiting for transfers between devices: 288 us -> 2.31 us
  blocking collectives: 31.1 us -> 86.6 us
  starting transfers between devices: 0.08 us -> 14.3 us
  between operations: 14.8 us -> 0.82 us
  other arithmetic: 1.34 us -> 10.1 us
  local copies, waits for them, and re-layouts: 12.1 us -> 7.62 us
    unnamed x3 -> x0, waiting for transfers between devices: 204 us -> none
    all_to_all x0 -> x4, blocking collectives: none -> 86.6 us  [the longest x3 56.4 us: spread(): lax.all_to_all(jnp.broadcast_to(block[None], (n,) + block.shape), axes, 0...]
    all_gather x1 -> x0, waiting for transfers between devices: 84.2 us -> none  [per_device(): all_rows = lax.all_gather(wide_rows, 'dp', axis=0, tiled=True)]
    psum x1 -> x0, blocking collectives: 21.1 us -> none  [per_device(): projected = lax.psum(partial_proj, 'fsdp')]
    ppermute x0 -> x2, starting transfers between devices: none -> 14.3 us  [the longest x1 7.51 us: per_device(): theirs = lax.ppermute(grad[half:], 'c', swap)]
    all_gather x1 -> x0, blocking collectives: 9.94 us -> none  [per_device(): wide_rows = lax.all_gather(direction, 'fsdp', axis=1, tiled=True)]
    concatenate x0 -> x1, other arithmetic: none -> 8.77 us  [per_device(): return (jnp.concatenate(update, axis=1), new_first, new_second)]
    unnamed x11 -> x9, local copies, waits for them, and re-layouts: 12.1 us -> 7.11 us
  transfers between devices with their start and end apart: 2 -> 2, of which waited for: 2 -> 2; matrix products, arithmetic and copies ran while one was open for 0% -> 1% of each run, Pallas kernels for 0% -> 0%
where the time goes in v1:
time: 129 us; the launch traced here: 128 us
  blocking collectives  86.6 us (67%)
  starting transfers between devices  14.3 us (11%)
  other arithmetic  10.1 us (8%)
  local copies, waits for them, and re-layouts  7.62 us (6%)
  matrix products  6.4 us (5%)
  waiting for transfers between devices  2.31 us (2%)
    all_to_all x3, blocking collectives, spread(): lax.all_to_all(jnp.broadcast_to(block[None], (n,) + block.shape), axes, 0...  56.4 us
    all_to_all x1, blocking collectives, per_device(): lax.all_to_all(chip, ('y', 'z'), 0, 0).astype(F32)  30.2 us
    concatenate x1, other arithmetic, per_device(): return (jnp.concatenate(update, axis=1), new_first, new_second)  8.77 us
    ppermute x1, starting transfers between devices, per_device(): theirs = lax.ppermute(grad[half:], 'c', swap)  7.51 us
    unnamed x9, local copies, waits for them, and re-layouts  7.11 us
    ppermute x1, starting transfers between devices, per_device(): other = lax.ppermute(mine, 'c', swap)  6.82 us
  transfers between devices with their start and end apart: 2, of which 2 were waited for; matrix products, arithmetic and copies ran while one was open for 1% of the time, Pallas kernels for 0%

profile of v1, /device:TPU:1, one launch (start us, length us, event | category | flops | bytes accessed | tf_op | source)
XLA Modules:
  0.0 128.1 jit_solution(5297590570006038259)
XLA Ops:
  0.7 1.0 copy-done
  1.7 0.6 convolution_convert_fusion
  2.8 0.5 fusion
  3.4 20.7 %all_to_all.20 = bf16[4,384,512]{2,1,0:T(8,128)(2,1)S(1)} all-to-all(bf16[4,384,512]{2,1,0:T(8,128)(2,1)S(1)} %broadcast_in_dim.8), channel_id=1, replica_groups=mesh['y'=8,'z'=8,'c'=2,'x'=4] {'x'}, dimensions={0} | all-to-all | bytes 3145728 | tf_op jit(solution)/shard_map/all_to_all | solution.py:12
  24.1 0.4 reduce_sum.21
  24.5 1.6 %fusion.64 = f32[512,640]{1,0:T(8,128)S(1)} fusion(bf16[384,512]{1,0:T(8,128)(2,1)S(1)} %reduce_sum.21, bf16[384,640]{1,0:T(8,128)(2,1)} %param.6), kind=kOutput, calls=%fused_computation.97 | convolution fusion | flops 251658240 | bytes 2195456 | tf_op jit(solution)/shard_map/dot_general | solution.py:31
  26.2 7.5 %collective-permute-start = (f32[256,640]{1,0:T(8,128)S(1)}, f32[256,640]{1,0:T(8,128)S(1)}, u32[]{:S(2)}, u32[]{:S(2)}) collective-permute-start(f32[256,640]{1,0:T(8,128)S(1)} %slice.56), channel_id=1, source_target_pairs={{0,4},{4,0},{1,5},{5,1},{2,6},{6,2},{3,7},{7,3},{8,12},{12,8},{9,1... | collective-permute-start | bytes 1966088 | tf_op jit(solution)/shard_map/ppermute | solution.py:34
  33.8 1.7 %collective-permute-done = f32[256,640]{1,0:T(8,128)S(1)} collective-permute-done((f32[256,640]{1,0:T(8,128)S(1)}, f32[256,640]{1,0:T(8,128)S(1)}, u32[]{:S(2)}, u32[]{:S(2)}) %collective-permute-start) | collective-permute-done | bytes 655392 | tf_op jit(solution)/shard_map/ppermute | solution.py:34
  35.6 30.2 %all_to_all.21 = bf16[64,4,640]{2,1,0:T(4,128)(2,1)S(1)} all-to-all(bf16[64,4,640]{2,1,0:T(4,128)(2,1)S(1)} %reshape.12), channel_id=1, replica_groups=mesh['y'=8,'z'=8,'c'=2,'x'=4] {'y','z'}, dimensions={0} | all-to-all | bytes 655360 | tf_op jit(solution)/shard_map/all_to_all | solution.py:36
  66.0 0.6 fusion.45
  66.7 19.1 %all_to_all.22 = bf16[64,4,640]{2,1,0:T(4,128)(2,1)S(1)} all-to-all(bf16[64,4,640]{2,1,0:T(4,128)(2,1)S(1)} %broadcast_in_dim.9), channel_id=1, replica_groups=mesh['y'=8,'z'=8,'c'=2,'x'=4] {'y','z'}, dimensions={0} | all-to-all | bytes 655360 | tf_op jit(solution)/shard_map/all_to_all | solution.py:12
  86.0 16.5 %all_to_all.23 = bf16[4,256,640]{2,1,0:T(8,128)(2,1)S(1)} all-to-all(bf16[4,256,640]{2,1,0:T(8,128)(2,1)S(1)} %broadcast_in_dim.22), channel_id=1, replica_groups=mesh['y'=8,'z'=8,'c'=2,'x'=4] {'x'}, dimensions={0} | all-to-all | bytes 2621440 | tf_op jit(solution)/shard_map/all_to_all | solution.py:12
  102.5 6.8 %collective-permute-start.1 = (bf16[4,256,640]{2,1,0:T(8,128)(2,1)S(1)}, bf16[4,256,640]{2,1,0:T(8,128)(2,1)S(1)}, u32[]{:S(2)}, u32[]{:S(2)}) collective-permute-start(bf16[4,256,640]{2,1,0:T(8,128)(2,1)S(1)} %all_to_all.23), channel_id=1, source_target_pairs={{0,4},{4,0},{1,5},{5,1},{2,6},{6,2},{3,7},{7,3},{8,12},{12,8},{9,1... | collective-permute-start | bytes 3932168 | tf_op jit(solution)/shard_map/ppermute | solution.py:46
  109.4 0.5 fusion.32
  109.8 0.5 fusion.33
  110.3 0.5 fusion.34
  110.8 0.5 fusion.35
  111.2 0.6 collective-permute-done.1
  111.8 0.5 add_convert_fusion
  112.3 0.5 add_convert_fusion.1
  112.8 0.5 add_convert_fusion.2
  113.2 0.5 add_convert_fusion.3
  113.7 8.8 %pad_maximum_fusion = bf16[640,2560]{0,1:T(8,128)(2,1)} fusion(bf16[640,640]{0,1:T(8,128)(2,1)S(1)} %add_convert_fusion, bf16[640,640]{0,1:T(8,128)(2,1)S(1)} %add_convert_fusion.1, bf16[640,640]{0,1:T(8,128)(2,1)S(1)} %add_convert_fusion.2, bf16[640,640]{0,1:T(8,128)(2,1)S(1)} %add_convert_fusion.3), kind=kLoop, calls=%fused_computation | loop fusion | flops 13107200 | bytes 6553600 | tf_op jit(solution)/shard_map/concatenate | solution.py:54
  122.5 5.7 %copy.10 = bf16[640,2560]{1,0:T(8,128)(2,1)} copy(bf16[640,2560]{0,1:T(8,128)(2,1)} %pad_maximum_fusion) | data formatting | bytes 6553600
  (20 shorter events, 1.2 us)
Async XLA Ops:
  0.6 1.1 copy-start
  1.7 1.0 copy-start.1
  26.2 39.8 %copy-start.2 = (f32[4,640]{1,0:T(4,128)S(1)}, f32[4,640]{1,0:T(4,128)}, u32[]{:S(2)}) copy-start(f32[4,640]{1,0:T(4,128)} %param.8) | copy-start | bytes 30724
  26.2 39.8 %copy-start.3 = (f32[4,640]{1,0:T(4,128)S(1)}, f32[4,640]{1,0:T(4,128)}, u32[]{:S(2)}) copy-start(f32[4,640]{1,0:T(4,128)} %param.9) | copy-start | bytes 30724
  26.2 9.2 %collective-permute-start = (f32[256,640]{1,0:T(8,128)S(1)}, f32[256,640]{1,0:T(8,128)S(1)}, u32[]{:S(2)}, u32[]{:S(2)}) collective-permute-start(f32[256,640]{1,0:T(8,128)S(1)} %slice.56), channel_id=1, source_target_pairs={{0,4},{4,0},{1,5},{5,1},{2,6},{6,2},{3,7},{7,3},{8,12},{12,8},{9,1... | collective-permute-start | bytes 1966088 | tf_op jit(solution)/shard_map/ppermute | solution.py:34
  102.5 9.3 %collective-permute-start.1 = (bf16[4,256,640]{2,1,0:T(8,128)(2,1)S(1)}, bf16[4,256,640]{2,1,0:T(8,128)(2,1)S(1)}, u32[]{:S(2)}, u32[]{:S(2)}) collective-permute-start(bf16[4,256,640]{2,1,0:T(8,128)(2,1)S(1)} %all_to_all.23), channel_id=1, source_target_pairs={{0,4},{4,0},{1,5},{5,1},{2,6},{6,2},{3,7},{7,3},{8,12},{12,8},{9,1... | collective-permute-start | bytes 3932168 | tf_op jit(solution)/shard_map/ppermute | solution.py:46

commit v2 on v1

v2 whole, which is shorter than its diff:
```python
import jax
import jax.numpy as jnp
from jax import lax
from jax.experimental import pallas as pl
from jax.experimental.pallas import tpu as pltpu
from jax.sharding import Mesh, PartitionSpec as P

STEP = 10
F32 = jnp.float32
BF16 = jnp.bfloat16


def spread(block, axes, n):
    return lax.all_to_all(jnp.broadcast_to(block[None], (n,) + block.shape), axes, 0, 0)


def rank_order(rank, own, first):
    half = rank // 2
    old = lax.broadcasted_iota(jnp.int32, (rank, rank), 0)
    new = lax.broadcasted_iota(jnp.int32, (rank, rank), 1)
    side = (new // half + first) % 2
    return (old == (new % half) // own * (2 * own) + side * own + new % own).astype(BF16)


def expand_kernel(basis_ref, mine_ref, other_ref, out_ref):
    half = mine_ref.shape[0]
    acc = jnp.dot(basis_ref[:, :half], mine_ref[...], preferred_element_type=F32)
    acc += jnp.dot(basis_ref[:, half:], other_ref[...], preferred_element_type=F32)
    out_ref[...] = acc.astype(out_ref.dtype)


def expand(basis, mine, other):
    nx, half, cols = mine.shape
    rows = basis.shape[0]
    return pl.pallas_call(
        expand_kernel,
        grid=(nx,),
        in_specs=[
            pl.BlockSpec((rows, 2 * half), lambda i: (0, 0)),
            pl.BlockSpec((None, half, cols), lambda i: (i, 0, 0)),
            pl.BlockSpec((None, half, cols), lambda i: (i, 0, 0)),
        ],
        out_specs=pl.BlockSpec((rows, cols), lambda i: (0, i)),
        out_shape=jax.ShapeDtypeStruct((rows, nx * cols), BF16),
        compiler_params=pltpu.CompilerParams(vmem_limit_bytes=24 * 1024 * 1024),
        cost_estimate=pl.CostEstimate(
            flops=4 * rows * half * nx * cols, bytes_accessed=10 * 1024 * 1024, transcendentals=0
        ),
    )(basis, mine, other)


def per_device(ny, nz, nx, inputs, out_grad, basis, moment_first, moment_second):
    rank = basis.shape[1]
    tokens = inputs.shape[0]
    groups = ny * nz
    own, cols = moment_first.shape
    half = rank // 2
    core = lax.axis_index("c")
    swap = [(0, 1), (1, 0)]

    partial = jnp.dot(inputs, basis, preferred_element_type=F32).astype(BF16)
    parts = lax.all_to_all(partial.reshape(nx, tokens // nx, rank), "x", 0, 0)

    theirs = lax.ppermute(out_grad, "c", swap)
    grads = jnp.where(
        core == 0, jnp.concatenate([out_grad, theirs]), jnp.concatenate([theirs, out_grad])
    )
    basis = jnp.dot(basis, rank_order(rank, own, core), preferred_element_type=F32).astype(BF16)

    projected = jnp.sum(parts.astype(F32), axis=0).astype(BF16)
    ordered = jnp.dot(projected, rank_order(rank, own, 0), preferred_element_type=F32).astype(BF16)
    sides = ordered.reshape(tokens // nx, 2, half).transpose(1, 0, 2)
    sides = jnp.broadcast_to(sides[:, None], (2, nx, tokens // nx, half)).reshape(2 * nx, tokens // nx, half)
    rows = lax.all_to_all(sides, ("c", "x"), 0, 0).reshape(2 * tokens, half)
    chip = lax.dot_general(rows, grads, (((0,), (0,)), ((), ())), preferred_element_type=F32)
    chip = chip.astype(BF16).reshape(groups, own, cols)
    grad_shard = jnp.sum(lax.all_to_all(chip, ("y", "z"), 0, 0).astype(F32), axis=0)

    new_first = 0.9 * moment_first + 0.1 * grad_shard
    new_second = 0.999 * moment_second + 0.001 * grad_shard * grad_shard
    corrected = new_first / (1.0 - 0.9**STEP)
    scaled = jnp.sqrt(new_second / (1.0 - 0.999**STEP)) + 1e-08
    direction = (corrected / scaled).astype(BF16)

    gathered = spread(direction, ("y", "z"), groups).reshape(half, cols)
    mine = spread(gathered, "x", nx)
    other = lax.ppermute(mine, "c", swap)
    return (expand(basis, mine, other), new_first, new_second)


def solution(mesh):
    ny, nz, nx = 8, 8, mesh.devices.shape[1]
    split = Mesh(mesh.devices.reshape(ny, nz, 2, nx), ("y", "z", "c", "x"))
    dp = ("y", "z", "c")

    def body(*args):
        return per_device(ny, nz, nx, *args)

    return jax.shard_map(
        body,
        mesh=split,
        in_specs=(P(dp, "x"), P(dp, "x"), P("x", None), P(dp, "x"), P(dp, "x")),
        out_specs=(P("x", None), P(dp, "x"), P(dp, "x")),
        check_vma=False,
    )
```

time: 129 us -> 112 us (0.87)
  blocking collectives: 86.6 us -> 62 us
  starting transfers between devices: 14.3 us -> 27.6 us
  other arithmetic: 10.1 us -> 0.87 us
  waiting for transfers between devices: 2.31 us -> 10 us
  local copies, waits for them, and re-layouts: 7.62 us -> 2.25 us
  Pallas kernels: 0 us -> 3.83 us
  matrix products: 6.4 us -> 3.7 us
    all_to_all x3 -> x2, blocking collectives: 56.4 us -> 35.7 us  [spread(): lax.all_to_all(jnp.broadcast_to(block[None], (n,) + block.shape), axes, 0...]
    all_to_all x0 -> x2, starting transfers between devices: none -> 13.6 us  [the longest x1 8.72 us: per_device(): rows = lax.all_to_all(sides, ('c', 'x'), 0, 0).reshape(2 * tokens, half)]
    concatenate x1 -> x0, other arithmetic: 8.77 us -> none  [per_device(): return (jnp.concatenate(update, axis=1), new_first, new_second)]
    all_to_all x0 -> x2, waiting for transfers between devices: none -> 7.97 us  [the longest x1 7.96 us: per_device(): rows = lax.all_to_all(sides, ('c', 'x'), 0, 0).reshape(2 * tokens, half)]
    unnamed x9 -> x8, local copies, waits for them, and re-layouts: 7.11 us -> 1.09 us
    dot_general x10 -> x3, matrix products: 5.9 us -> 1.45 us  [the longest x1 0.58 us: per_device(): jnp.dot(basis, rank_order(rank, own, core), preferred_element_type=F32)]
    pallas_call x0 -> x1, Pallas kernels: none -> 3.83 us  [expand(): pl.pallas_call(expand_kernel, grid=(nx,), in_specs=[pl.BlockSpec((rows, 2...]
    all_to_all x1, blocking collectives: 30.2 us -> 26.4 us  [per_device(): lax.all_to_all(chip, ('y', 'z'), 0, 0).astype(F32)]
  transfers between devices with their start and end apart: 2 -> 4, of which waited for: 2 -> 2; matrix products, arithmetic and copies ran while one was open for 1% -> 2% of each run, Pallas kernels for 0% -> 0%
where the time goes in v2:
time: 112 us; the launch traced here: 111 us
  blocking collectives  62 us (55%)
  starting transfers between devices  27.6 us (25%)
  waiting for transfers between devices  10 us (9%)
  Pallas kernels  3.83 us (3%)
  matrix products  3.7 us (3%)
  local copies, waits for them, and re-layouts  2.25 us (2%)
    all_to_all x2, blocking collectives, spread(): lax.all_to_all(jnp.broadcast_to(block[None], (n,) + block.shape), axes, 0...  35.7 us
    all_to_all x1, blocking collectives, per_device(): lax.all_to_all(chip, ('y', 'z'), 0, 0).astype(F32)  26.4 us
    all_to_all x1, starting transfers between devices, per_device(): rows = lax.all_to_all(sides, ('c', 'x'), 0, 0).reshape(2 * tokens, half)  8.72 us
    all_to_all x1, waiting for transfers between devices, per_device(): rows = lax.all_to_all(sides, ('c', 'x'), 0, 0).reshape(2 * tokens, half)  7.96 us
    ppermute x1, starting transfers between devices, per_device(): theirs = lax.ppermute(out_grad, 'c', swap)  7.42 us
    ppermute x1, starting transfers between devices, per_device(): other = lax.ppermute(mine, 'c', swap)  6.64 us
    all_to_all x1, starting transfers between devices, per_device(): parts = lax.all_to_all(partial.reshape(nx, tokens // nx, rank), 'x', 0, 0)  4.84 us
    pallas_call x1, Pallas kernels, expand(): pl.pallas_call(expand_kernel, grid=(nx,), in_specs=[pl.BlockSpec((rows, 2...  3.83 us
  transfers between devices with their start and end apart: 4, of which 2 were waited for; matrix products, arithmetic and copies ran while one was open for 2% of the time, Pallas kernels for 0%

profile of v2, /device:TPU:1, one launch (start us, length us, event | category | flops | bytes accessed | tf_op | source)
XLA Modules:
  0.0 111.1 jit_solution(7298144298677413911)
XLA Ops:
  0.6 0.0 copy-start
  0.7 1.1 copy-done
  1.7 2.2 %convolution_convert_fusion.1 = bf16[384,512]{1,0:T(8,128)(2,1)} fusion(bf16[384,640]{1,0:T(8,128)(2,1)} %param.5, bf16[640,512]{1,0:T(8,128)(2,1)S(1)} %copy-done), kind=kOutput, calls=%fused_computation.22 | convolution fusion | flops 251854848 | bytes 1540096 | tf_op jit(solution)/shard_map/dot_general | solution.py:61
  4.0 4.8 %all-to-all-start = ((bf16[4,96,512]{2,1,0:T(8,128)(2,1)}), bf16[4,96,512]{2,1,0:T(8,128)(2,1)S(1)}, u32[]{:S(2)}, u32[]{:S(2)}) async-start(bf16[4,96,512]{2,1,0:T(8,128)(2,1)} %bitcast.1), calls=%async_computation | async-start | bytes 786432 | tf_op jit(solution)/shard_map/all_to_all | solution.py:62
  8.8 7.4 %collective-permute-start = (bf16[384,640]{1,0:T(8,128)(2,1)S(1)}, bf16[384,640]{1,0:T(8,128)(2,1)S(1)}, u32[]{:S(2)}, u32[]{:S(2)}) collective-permute-start(bf16[384,640]{1,0:T(8,128)(2,1)S(1)} %copy-done.3), channel_id=1, source_target_pairs={{0,4},{4,0},{1,5},{5,1},{2,6},{6,2},{3,7},{7,3},{8,12},{12,8},{9,1... | collective-permute-start | bytes 1474568 | tf_op jit(solution)/shard_map/ppermute | solution.py:64
  16.3 0.1 reduce_sum.21
  16.4 0.3 convolution_convert_fusion.3
  16.8 0.8 broadcast_in_dim.8
  17.6 8.7 %all-to-all-start.1 = ((bf16[8,96,256]{2,1,0:T(8,128)(2,1)}), bf16[8,96,256]{2,1,0:T(8,128)(2,1)S(1)}, u32[]{:S(2)}, u32[]{:S(2)}) async-start(bf16[8,96,256]{2,1,0:T(8,128)(2,1)} %bitcast.3), calls=%async_computation.1 | async-start | bytes 786432 | tf_op jit(solution)/shard_map/all_to_all | solution.py:74
  26.3 8.0 %all-to-all-done.1 = bf16[8,96,256]{2,1,0:T(8,128)(2,1)S(1)} async-done(((bf16[8,96,256]{2,1,0:T(8,128)(2,1)}), bf16[8,96,256]{2,1,0:T(8,128)(2,1)S(1)}, u32[]{:S(2)}, u32[]{:S(2)}) %all-to-all-start.1) | async-done | bytes 393248 | tf_op jit(solution)/shard_map/all_to_all | solution.py:74
  34.3 0.5 convolution_convert_fusion.2
  34.8 0.1 reshape.28
  34.9 26.4 %all_to_all.25 = bf16[64,4,640]{2,1,0:T(4,128)(2,1)S(1)} all-to-all(bf16[64,4,640]{2,1,0:T(4,128)(2,1)S(1)} %reshape.28), channel_id=1, replica_groups=mesh['y'=8,'z'=8,'c'=2,'x'=4] {'y','z'}, dimensions={0} | all-to-all | bytes 655360 | tf_op jit(solution)/shard_map/all_to_all | solution.py:77
  61.2 0.2 convert_reduce_fusion
  61.4 0.6 fusion.53
  62.0 0.1 broadcast_in_dim.9
  62.1 19.1 %all_to_all.26 = bf16[64,4,640]{2,1,0:T(4,128)(2,1)S(1)} all-to-all(bf16[64,4,640]{2,1,0:T(4,128)(2,1)S(1)} %broadcast_in_dim.9), channel_id=1, replica_groups=mesh['y'=8,'z'=8,'c'=2,'x'=4] {'y','z'}, dimensions={0} | all-to-all | bytes 655360 | tf_op jit(solution)/shard_map/all_to_all | solution.py:14
  81.2 0.1 broadcast_in_dim.10
  81.3 0.1 broadcast_in_dim.22
  81.4 16.5 %all_to_all.27.mine_ref = bf16[4,256,640]{2,1,0:T(8,128)(2,1)S(1)} all-to-all(bf16[4,256,640]{2,1,0:T(8,128)(2,1)S(1)} %broadcast_in_dim.22), channel_id=1, replica_groups=mesh['y'=8,'z'=8,'c'=2,'x'=4] {'x'}, dimensions={0} | all-to-all | bytes 2621440 | tf_op jit(solution)/shard_map/all_to_all | solution.py:14
  98.0 6.6 %collective-permute-start.1 = (bf16[4,256,640]{2,1,0:T(8,128)(2,1)S(1)}, bf16[4,256,640]{2,1,0:T(8,128)(2,1)S(1)}, u32[]{:S(2)}, u32[]{:S(2)}) collective-permute-start(bf16[4,256,640]{2,1,0:T(8,128)(2,1)S(1)} %all_to_all.27.mine_ref), channel_id=1, source_target_pairs={{0,4},{4,0},{1,5},{5,1},{2,6},{6,2},{3,7},{7,3},{8,12},{12,8},{9,1... | collective-permute-start | bytes 3932168 | tf_op jit(solution)/shard_map/ppermute | solution.py:87
  104.6 0.6 fusion.3.basis_ref
  105.2 2.0 %collective-permute-done.1.other_ref = bf16[4,256,640]{2,1,0:T(8,128)(2,1)S(1)} collective-permute-done((bf16[4,256,640]{2,1,0:T(8,128)(2,1)S(1)}, bf16[4,256,640]{2,1,0:T(8,128)(2,1)S(1)}, u32[]{:S(2)}, u32[]{:S(2)}) %collective-permute-start.1) | collective-permute-done | bytes 1310752 | tf_op jit(solution)/shard_map/ppermute | solution.py:87
  107.3 3.8 %shard_map.76 = bf16[640,2560]{1,0:T(8,128)(2,1)} custom-call(bf16[640,512]{1,0:T(8,128)(2,1)S(1)} %fusion.3.basis_ref, bf16[4,256,640]{2,1,0:T(8,128)(2,1)S(1)} %all_to_all.27.mine_ref, bf16[4,256,640]{2,1,0:T(8,128)(2,1)S(1)} %collective-permute-done.1.other_ref), custom_call_target="tpu_custom_call" | custom-call | flops 1677721600 | bytes 10485760 | tf_op jit(solution)/shard_map/pallas_call | solution.py:35
  (15 shorter events, 0.1 us)
Async XLA Ops:
  0.6 1.1 copy-start
  0.6 8.2 %copy-start.3 = (bf16[384,640]{1,0:T(8,128)(2,1)S(1)}, bf16[384,640]{1,0:T(8,128)(2,1)}, u32[]{:S(2)}) copy-start(bf16[384,640]{1,0:T(8,128)(2,1)} %param.6) | copy-start | bytes 1474564
  4.0 12.3 %all-to-all-start = ((bf16[4,96,512]{2,1,0:T(8,128)(2,1)}), bf16[4,96,512]{2,1,0:T(8,128)(2,1)S(1)}, u32[]{:S(2)}, u32[]{:S(2)}) async-start(bf16[4,96,512]{2,1,0:T(8,128)(2,1)} %bitcast.1), calls=%async_computation | async-start | bytes 786432 | tf_op jit(solution)/shard_map/all_to_all | solution.py:62
  8.8 17.5 %collective-permute-start = (bf16[384,640]{1,0:T(8,128)(2,1)S(1)}, bf16[384,640]{1,0:T(8,128)(2,1)S(1)}, u32[]{:S(2)}, u32[]{:S(2)}) collective-permute-start(bf16[384,640]{1,0:T(8,128)(2,1)S(1)} %copy-done.3), channel_id=1, source_target_pairs={{0,4},{4,0},{1,5},{5,1},{2,6},{6,2},{3,7},{7,3},{8,12},{12,8},{9,1... | collective-permute-start | bytes 1474568 | tf_op jit(solution)/shard_map/ppermute | solution.py:64
  17.6 16.7 %all-to-all-start.1 = ((bf16[8,96,256]{2,1,0:T(8,128)(2,1)}), bf16[8,96,256]{2,1,0:T(8,128)(2,1)S(1)}, u32[]{:S(2)}, u32[]{:S(2)}) async-start(bf16[8,96,256]{2,1,0:T(8,128)(2,1)} %bitcast.3), calls=%async_computation.1 | async-start | bytes 786432 | tf_op jit(solution)/shard_map/all_to_all | solution.py:74
  34.3 27.2 %copy-start.1 = (f32[4,640]{1,0:T(4,128)S(1)}, f32[4,640]{1,0:T(4,128)}, u32[]{:S(2)}) copy-start(f32[4,640]{1,0:T(4,128)} %param.8) | copy-start | bytes 30724
  34.3 27.2 %copy-start.2 = (f32[4,640]{1,0:T(4,128)S(1)}, f32[4,640]{1,0:T(4,128)}, u32[]{:S(2)}) copy-start(f32[4,640]{1,0:T(4,128)} %param.9) | copy-start | bytes 30724
  98.0 9.3 %collective-permute-start.1 = (bf16[4,256,640]{2,1,0:T(8,128)(2,1)S(1)}, bf16[4,256,640]{2,1,0:T(8,128)(2,1)S(1)}, u32[]{:S(2)}, u32[]{:S(2)}) collective-permute-start(bf16[4,256,640]{2,1,0:T(8,128)(2,1)S(1)} %all_to_all.27.mine_ref), channel_id=1, source_target_pairs={{0,4},{4,0},{1,5},{5,1},{2,6},{6,2},{3,7},{7,3},{8,12},{12,8},{9,1... | collective-permute-start | bytes 3932168 | tf_op jit(solution)/shard_map/ppermute | solution.py:87

commit v3 on v2

v3 whole, which is shorter than its diff:
```python
import functools

import jax
import jax.numpy as jnp
from jax import lax
from jax.experimental import pallas as pl
from jax.experimental.pallas import tpu as pltpu
from jax.sharding import Mesh, PartitionSpec as P

STEP = 10
F32 = jnp.float32
BF16 = jnp.bfloat16


def spread(block, axes, n):
    return lax.all_to_all(jnp.broadcast_to(block[None], (n,) + block.shape), axes, 0, 0)


def rank_order(rank, own, first):
    half = rank // 2
    old = lax.broadcasted_iota(jnp.int32, (rank, rank), 0)
    new = lax.broadcasted_iota(jnp.int32, (rank, rank), 1)
    side = (new // half + first) % 2
    return (old == (new % half) // own * (2 * own) + side * own + new % own).astype(BF16)


def whole():
    return pl.BlockSpec(memory_space=pltpu.VMEM)


def project_kernel(inputs_ref, basis_ref, out_ref):
    out_ref[...] = jnp.dot(inputs_ref[...], basis_ref[...], preferred_element_type=F32).astype(BF16)


def project(inputs, basis):
    return pl.pallas_call(
        project_kernel,
        in_specs=[whole(), whole()],
        out_specs=whole(),
        out_shape=jax.ShapeDtypeStruct((inputs.shape[0], basis.shape[1]), BF16),
        compiler_params=pltpu.CompilerParams(vmem_limit_bytes=16 * 1024 * 1024),
    )(inputs, basis)


def combine_kernel(own, parts_ref, out_ref):
    nx, _, rank = parts_ref.shape
    half = rank // 2
    total = parts_ref[0].astype(F32)
    for i in range(1, nx):
        total += parts_ref[i].astype(F32)
    total = total.astype(BF16)
    old = lax.broadcasted_iota(jnp.int32, (rank, half), 0)
    new = lax.broadcasted_iota(jnp.int32, (rank, half), 1)
    for c in range(2):
        pick = (old == new // own * (2 * own) + c * own + new % own).astype(F32).astype(BF16)
        side = jnp.dot(total, pick, preferred_element_type=F32).astype(BF16)
        for i in range(nx):
            out_ref[c * nx + i] = side


def combine(parts, own):
    nx, tokens, rank = parts.shape
    return pl.pallas_call(
        functools.partial(combine_kernel, own),
        in_specs=[whole()],
        out_specs=whole(),
        out_shape=jax.ShapeDtypeStruct((2 * nx, tokens, rank // 2), BF16),
        compiler_params=pltpu.CompilerParams(vmem_limit_bytes=16 * 1024 * 1024),
    )(parts)


def expand_mine_kernel(basis_ref, mine_ref, out_ref):
    nx, half, _ = mine_ref.shape
    for i in range(nx):
        out_ref[i] = jnp.dot(basis_ref[:, :half], mine_ref[i], preferred_element_type=F32)


def expand_mine(basis, mine):
    nx, half, cols = mine.shape
    rows = basis.shape[0]
    return pl.pallas_call(
        expand_mine_kernel,
        in_specs=[whole(), whole()],
        out_specs=whole(),
        out_shape=jax.ShapeDtypeStruct((nx, rows, cols), F32),
        compiler_params=pltpu.CompilerParams(vmem_limit_bytes=24 * 1024 * 1024),
        cost_estimate=pl.CostEstimate(
            flops=2 * rows * half * nx * cols, bytes_accessed=4 * nx * rows * cols, transcendentals=0
        ),
    )(basis, mine)


def expand_kernel(tiles, basis_ref, other_ref, mine_ref, out_ref, done, sems):
    nx, half, cols = other_ref.shape
    size = basis_ref.shape[0] // tiles
    copies = []
    for t in range(tiles):
        rows = pl.ds(t * size, size)
        for i in range(nx):
            acc = mine_ref[i, rows, :] + jnp.dot(
                basis_ref[rows, half:], other_ref[i], preferred_element_type=F32
            )
            done[rows, pl.ds(i * cols, cols)] = acc.astype(BF16)
        copies.append(pltpu.make_async_copy(done.at[rows], out_ref.at[rows], sems.at[t]))
        copies[-1].start()
    for copy in copies:
        copy.wait()


def expand(basis, other, mine, tiles=5):
    nx, half, cols = other.shape
    rows = basis.shape[0]
    return pl.pallas_call(
        functools.partial(expand_kernel, tiles),
        in_specs=[whole(), whole(), whole()],
        out_specs=pl.BlockSpec(memory_space=pl.ANY),
        out_shape=jax.ShapeDtypeStruct((rows, nx * cols), BF16),
        scratch_shapes=[pltpu.VMEM((rows, nx * cols), BF16), pltpu.SemaphoreType.DMA((tiles,))],
        compiler_params=pltpu.CompilerParams(vmem_limit_bytes=24 * 1024 * 1024),
    )(basis, other, mine)


def per_device(ny, nz, nx, inputs, out_grad, basis, moment_first, moment_second):
    rank = basis.shape[1]
    tokens = inputs.shape[0]
    groups = ny * nz
    own, cols = moment_first.shape
    half = rank // 2
    core = lax.axis_index("c")
    swap = [(0, 1), (1, 0)]

    partial = project(inputs, basis)
    parts = lax.all_to_all(partial.reshape(nx, tokens // nx, rank), "x", 0, 0)

    theirs = lax.ppermute(out_grad, "c", swap)
    grads = jnp.where(
        core == 0, jnp.concatenate([out_grad, theirs]), jnp.concatenate([theirs, out_grad])
    )
    basis = jnp.dot(basis, rank_order(rank, own, core), preferred_element_type=F32).astype(BF16)
    sides, basis = lax.optimization_barrier((combine(parts, own), basis))
    rows = lax.all_to_all(sides, ("c", "x"), 0, 0).reshape(2 * tokens, half)
    chip = lax.dot_general(rows, grads, (((0,), (0,)), ((), ())), preferred_element_type=F32)
    chip = chip.astype(BF16).reshape(groups, own, cols)
    grad_shard = jnp.sum(lax.all_to_all(chip, ("y", "z"), 0, 0).astype(F32), axis=0)

    new_first = 0.9 * moment_first + 0.1 * grad_shard
    new_second = 0.999 * moment_second + 0.001 * grad_shard * grad_shard
    corrected = new_first / (1.0 - 0.9**STEP)
    scaled = jnp.sqrt(new_second / (1.0 - 0.999**STEP)) + 1e-08
    direction = (corrected / scaled).astype(BF16)

    gathered = spread(direction, ("y", "z"), groups).reshape(half, cols)
    mine = spread(gathered, "x", nx)
    other = lax.ppermute(mine, "c", swap)
    return (expand(basis, other, expand_mine(basis, mine)), new_first, new_second)


def solution(mesh):
    ny, nz, nx = 8, 8, mesh.devices.shape[1]
    split = Mesh(mesh.devices.reshape(ny, nz, 2, nx), ("y", "z", "c", "x"))
    dp = ("y", "z", "c")

    def body(*args):
        return per_device(ny, nz, nx, *args)

    return jax.shard_map(
        body,
        mesh=split,
        in_specs=(P(dp, "x"), P(dp, "x"), P("x", None), P(dp, "x"), P(dp, "x")),
        out_specs=(P("x", None), P(dp, "x"), P(dp, "x")),
        check_vma=False,
    )
```

time: 112 us -> 110 us (0.982)
  matrix products: 3.7 us -> 1.1 us
  Pallas kernels: 3.83 us -> 5.54 us
    dot_general x2 -> x0, matrix products: 2.59 us -> none  [the longest x1 2.24 us: per_device(): partial = jnp.dot(inputs, basis, preferred_element_type=F32).astype(BF16)]
    pallas_call x1 -> x4, Pallas kernels: 3.83 us -> 5.54 us  [the longest x1 2.12 us: expand(): pl.pallas_call(functools.partial(expand_kernel, tiles), in_specs=[whole()...]
  transfers between devices with their start and end apart: 4 -> 4, of which waited for: 2 -> 2; matrix products, arithmetic and copies ran while one was open for 2% -> 1% of each run, Pallas kernels for 0% -> 2%
where the time goes in v3:
time: 110 us; the launch traced here: 109 us
  blocking collectives  62 us (56%)
  starting transfers between devices  27 us (25%)
  waiting for transfers between devices  9.42 us (9%)
  Pallas kernels  5.54 us (5%)
  local copies, waits for them, and re-layouts  2.48 us (2%)
  matrix products  1.1 us (1%)
    all_to_all x2, blocking collectives, spread(): lax.all_to_all(jnp.broadcast_to(block[None], (n,) + block.shape), axes, 0...  35.7 us
    all_to_all x1, blocking collectives, per_device(): lax.all_to_all(chip, ('y', 'z'), 0, 0).astype(F32)  26.4 us
    all_to_all x1, starting transfers between devices, per_device(): rows = lax.all_to_all(sides, ('c', 'x'), 0, 0).reshape(2 * tokens, half)  8.12 us
    all_to_all x1, waiting for transfers between devices, per_device(): rows = lax.all_to_all(sides, ('c', 'x'), 0, 0).reshape(2 * tokens, half)  7.96 us
    ppermute x1, starting transfers between devices, per_device(): theirs = lax.ppermute(out_grad, 'c', swap)  7.42 us
    ppermute x1, starting transfers between devices, per_device(): other = lax.ppermute(mine, 'c', swap)  6.64 us
    all_to_all x1, starting transfers between devices, per_device(): parts = lax.all_to_all(partial.reshape(nx, tokens // nx, rank), 'x', 0, 0)  4.84 us
  transfers between devices with their start and end apart: 4, of which 2 were waited for; matrix products, arithmetic and copies ran while one was open for 1% of the time, Pallas kernels for 2%

profile of v3, /device:TPU:1, one launch (start us, length us, event | category | flops | bytes accessed | tf_op | source)
XLA Modules:
  0.0 109.2 jit_solution(11281254401773611375)
XLA Ops:
  0.6 1.1 copy-done
  1.7 1.0 copy-done.2
  2.8 1.2 %shard_map.76 = bf16[384,512]{1,0:T(8,128)(2,1)} custom-call(bf16[384,640]{1,0:T(8,128)(2,1)S(1)} %copy-done.2, bf16[640,512]{1,0:T(8,128)(2,1)S(1)} %copy-done), custom_call_target="tpu_custom_call" | custom-call | tf_op jit(solution)/shard_map/pallas_call | solution.py:36
  4.0 4.8 %all-to-all-start = ((bf16[4,96,512]{2,1,0:T(8,128)(2,1)}), bf16[4,96,512]{2,1,0:T(8,128)(2,1)S(1)}, u32[]{:S(2)}, u32[]{:S(2)}) async-start(bf16[4,96,512]{2,1,0:T(8,128)(2,1)} %bitcast), calls=%async_computation | async-start | bytes 786432 | tf_op jit(solution)/shard_map/all_to_all | solution.py:133
  8.8 7.4 %collective-permute-start = (bf16[384,640]{1,0:T(8,128)(2,1)S(1)}, bf16[384,640]{1,0:T(8,128)(2,1)S(1)}, u32[]{:S(2)}, u32[]{:S(2)}) collective-permute-start(bf16[384,640]{1,0:T(8,128)(2,1)S(1)} %copy-done.5), channel_id=1, source_target_pairs={{0,4},{4,0},{1,5},{5,1},{2,6},{6,2},{3,7},{7,3},{8,12},{12,8},{9,1... | collective-permute-start | bytes 1474568 | tf_op jit(solution)/shard_map/ppermute | solution.py:135
  16.3 0.6 fusion.basis_ref
  16.9 0.0 all-to-all-done.parts_ref
  16.9 1.0 shard_map.77
  17.9 8.1 %all-to-all-start.1 = ((bf16[8,96,256]{2,1,0:T(8,128)(2,1)}), bf16[8,96,256]{2,1,0:T(8,128)(2,1)S(1)}, u32[]{:S(2)}, u32[]{:S(2)}) async-start(bf16[8,96,256]{2,1,0:T(8,128)(2,1)} %shard_map.77), calls=%async_computation.1 | async-start | bytes 786432 | tf_op jit(solution)/shard_map/all_to_all | solution.py:141
  26.1 8.0 %all-to-all-done.1 = bf16[8,96,256]{2,1,0:T(8,128)(2,1)S(1)} async-done(((bf16[8,96,256]{2,1,0:T(8,128)(2,1)}), bf16[8,96,256]{2,1,0:T(8,128)(2,1)S(1)}, u32[]{:S(2)}, u32[]{:S(2)}) %all-to-all-start.1) | async-done | bytes 393248 | tf_op jit(solution)/shard_map/all_to_all | solution.py:141
  34.0 0.5 convolution_convert_fusion.1
  34.6 0.1 reshape.19
  34.6 26.4 %all_to_all.25 = bf16[64,4,640]{2,1,0:T(4,128)(2,1)S(1)} all-to-all(bf16[64,4,640]{2,1,0:T(4,128)(2,1)S(1)} %reshape.19), channel_id=1, replica_groups=mesh['y'=8,'z'=8,'c'=2,'x'=4] {'y','z'}, dimensions={0} | all-to-all | bytes 655360 | tf_op jit(solution)/shard_map/all_to_all | solution.py:144
  61.0 0.2 convert_reduce_fusion
  61.2 0.6 fusion.40
  61.8 0.1 broadcast_in_dim.6
  61.9 19.1 %all_to_all.26 = bf16[64,4,640]{2,1,0:T(4,128)(2,1)S(1)} all-to-all(bf16[64,4,640]{2,1,0:T(4,128)(2,1)S(1)} %broadcast_in_dim.6), channel_id=1, replica_groups=mesh['y'=8,'z'=8,'c'=2,'x'=4] {'y','z'}, dimensions={0} | all-to-all | bytes 655360 | tf_op jit(solution)/shard_map/all_to_all | solution.py:16
  81.0 0.1 broadcast_in_dim.14
  81.1 0.1 broadcast_in_dim.15
  81.2 16.5 %all_to_all.27.mine_ref = bf16[4,256,640]{2,1,0:T(8,128)(2,1)S(1)} all-to-all(bf16[4,256,640]{2,1,0:T(8,128)(2,1)S(1)} %broadcast_in_dim.15), channel_id=1, replica_groups=mesh['y'=8,'z'=8,'c'=2,'x'=4] {'x'}, dimensions={0} | all-to-all | bytes 2621440 | tf_op jit(solution)/shard_map/all_to_all | solution.py:16
  97.8 6.6 %collective-permute-start.1 = (bf16[4,256,640]{2,1,0:T(8,128)(2,1)S(1)}, bf16[4,256,640]{2,1,0:T(8,128)(2,1)S(1)}, u32[]{:S(2)}, u32[]{:S(2)}) collective-permute-start(bf16[4,256,640]{2,1,0:T(8,128)(2,1)S(1)} %all_to_all.27.mine_ref), channel_id=1, source_target_pairs={{0,4},{4,0},{1,5},{5,1},{2,6},{6,2},{3,7},{7,3},{8,12},{12,8},{9,1... | collective-permute-start | bytes 3932168 | tf_op jit(solution)/shard_map/ppermute | solution.py:154
  104.4 1.2 %shard_map.78.mine_ref = f32[4,640,640]{2,1,0:T(8,128)S(1)} custom-call(bf16[640,512]{1,0:T(8,128)(2,1)S(1)} %fusion.basis_ref, bf16[4,256,640]{2,1,0:T(8,128)(2,1)S(1)} %all_to_all.27.mine_ref), custom_call_target="tpu_custom_call" | custom-call | flops 838860800 | bytes 6553600 | tf_op jit(solution)/shard_map/pallas_call | solution.py:81
  105.6 1.4 %collective-permute-done.1.other_ref = bf16[4,256,640]{2,1,0:T(8,128)(2,1)S(1)} collective-permute-done((bf16[4,256,640]{2,1,0:T(8,128)(2,1)S(1)}, bf16[4,256,640]{2,1,0:T(8,128)(2,1)S(1)}, u32[]{:S(2)}, u32[]{:S(2)}) %collective-permute-start.1) | collective-permute-done | bytes 1310752 | tf_op jit(solution)/shard_map/ppermute | solution.py:154
  107.1 2.1 %shard_map.79 = bf16[640,2560]{1,0:T(8,128)(2,1)} custom-call(bf16[640,512]{1,0:T(8,128)(2,1)S(1)} %fusion.basis_ref, bf16[4,256,640]{2,1,0:T(8,128)(2,1)S(1)} %collective-permute-done.1.other_ref, f32[4,640,640]{2,1,0:T(8,128)S(1)} %shard_map.78.mine_ref), custom_call_target="tpu_custom_call" | custom-call | tf_op jit(solution)/shard_map/pallas_call | solution.py:113
  (16 shorter events, 0.0 us)
Async XLA Ops:
  0.6 1.1 copy-start
  1.7 1.0 copy-start.2
  2.7 6.1 %copy-start.5 = (bf16[384,640]{1,0:T(8,128)(2,1)S(1)}, bf16[384,640]{1,0:T(8,128)(2,1)}, u32[]{:S(2)}) copy-start(bf16[384,640]{1,0:T(8,128)(2,1)} %param.6) | copy-start | bytes 1474564
  2.8 13.6 %copy-start.1 = (bf16[640,512]{1,0:T(8,128)(2,1)S(1)}, bf16[640,512]{1,0:T(8,128)(2,1)}, u32[]{:S(2)}) copy-start(bf16[640,512]{1,0:T(8,128)(2,1)} %basis_ref.1) | copy-start | bytes 1966084
  4.0 12.9 %all-to-all-start = ((bf16[4,96,512]{2,1,0:T(8,128)(2,1)}), bf16[4,96,512]{2,1,0:T(8,128)(2,1)S(1)}, u32[]{:S(2)}, u32[]{:S(2)}) async-start(bf16[4,96,512]{2,1,0:T(8,128)(2,1)} %bitcast), calls=%async_computation | async-start | bytes 786432 | tf_op jit(solution)/shard_map/all_to_all | solution.py:133
  8.8 17.2 %collective-permute-start = (bf16[384,640]{1,0:T(8,128)(2,1)S(1)}, bf16[384,640]{1,0:T(8,128)(2,1)S(1)}, u32[]{:S(2)}, u32[]{:S(2)}) collective-permute-start(bf16[384,640]{1,0:T(8,128)(2,1)S(1)} %copy-done.5), channel_id=1, source_target_pairs={{0,4},{4,0},{1,5},{5,1},{2,6},{6,2},{3,7},{7,3},{8,12},{12,8},{9,1... | collective-permute-start | bytes 1474568 | tf_op jit(solution)/shard_map/ppermute | solution.py:135
  17.9 16.1 %all-to-all-start.1 = ((bf16[8,96,256]{2,1,0:T(8,128)(2,1)}), bf16[8,96,256]{2,1,0:T(8,128)(2,1)S(1)}, u32[]{:S(2)}, u32[]{:S(2)}) async-start(bf16[8,96,256]{2,1,0:T(8,128)(2,1)} %shard_map.77), calls=%async_computation.1 | async-start | bytes 786432 | tf_op jit(solution)/shard_map/all_to_all | solution.py:141
  34.0 27.2 %copy-start.3 = (f32[4,640]{1,0:T(4,128)S(1)}, f32[4,640]{1,0:T(4,128)}, u32[]{:S(2)}) copy-start(f32[4,640]{1,0:T(4,128)} %param.8) | copy-start | bytes 30724
  34.0 27.2 %copy-start.4 = (f32[4,640]{1,0:T(4,128)S(1)}, f32[4,640]{1,0:T(4,128)}, u32[]{:S(2)}) copy-start(f32[4,640]{1,0:T(4,128)} %param.9) | copy-start | bytes 30724
  97.8 9.3 %collective-permute-start.1 = (bf16[4,256,640]{2,1,0:T(8,128)(2,1)S(1)}, bf16[4,256,640]{2,1,0:T(8,128)(2,1)S(1)}, u32[]{:S(2)}, u32[]{:S(2)}) collective-permute-start(bf16[4,256,640]{2,1,0:T(8,128)(2,1)S(1)} %all_to_all.27.mine_ref), channel_id=1, source_target_pairs={{0,4},{4,0},{1,5},{5,1},{2,6},{6,2},{3,7},{7,3},{8,12},{12,8},{9,1... | collective-permute-start | bytes 3932168 | tf_op jit(solution)/shard_map/ppermute | solution.py:154

commit v4 on v3

v4 whole, which is shorter than its diff:
```python
import functools

import jax
import jax.numpy as jnp
from jax import lax
from jax.experimental import pallas as pl
from jax.experimental.pallas import tpu as pltpu
from jax.sharding import Mesh, PartitionSpec as P

STEP = 10
F32 = jnp.float32
BF16 = jnp.bfloat16


def spread(block, axes, n):
    return lax.all_to_all(jnp.broadcast_to(block[None], (n,) + block.shape), axes, 0, 0)


def whole():
    return pl.BlockSpec(memory_space=pltpu.VMEM)


def order_kernel(own, out_ref):
    _, rank, half = out_ref.shape
    old = lax.broadcasted_iota(jnp.int32, (rank, half), 0)
    new = lax.broadcasted_iota(jnp.int32, (rank, half), 1)
    for c in range(2):
        out_ref[c] = (old == new // own * (2 * own) + c * own + new % own).astype(F32).astype(BF16)


def rank_order(rank, own):
    return pl.pallas_call(
        functools.partial(order_kernel, own),
        in_specs=[],
        out_specs=whole(),
        out_shape=jax.ShapeDtypeStruct((2, rank, rank // 2), BF16),
        compiler_params=pltpu.CompilerParams(vmem_limit_bytes=16 * 1024 * 1024),
        cost_estimate=pl.CostEstimate(flops=4 * 10**9, bytes_accessed=8 * 10**6, transcendentals=0),
    )()


def project_kernel(inputs_ref, basis_ref, picks_ref, out_ref):
    del picks_ref
    out_ref[...] = jnp.dot(inputs_ref[...], basis_ref[...], preferred_element_type=F32).astype(BF16)


def project(inputs, basis, picks):
    return pl.pallas_call(
        project_kernel,
        in_specs=[whole(), whole(), whole()],
        out_specs=whole(),
        out_shape=jax.ShapeDtypeStruct((inputs.shape[0], basis.shape[1]), BF16),
        compiler_params=pltpu.CompilerParams(vmem_limit_bytes=16 * 1024 * 1024),
    )(inputs, basis, picks)


def combine_kernel(parts_ref, picks_ref, out_ref):
    nx = parts_ref.shape[0]
    total = parts_ref[0].astype(F32)
    for i in range(1, nx):
        total += parts_ref[i].astype(F32)
    total = total.astype(BF16)
    for c in range(2):
        side = jnp.dot(total, picks_ref[c], preferred_element_type=F32).astype(BF16)
        for i in range(nx):
            out_ref[c * nx + i] = side


def combine(parts, picks):
    nx, tokens, rank = parts.shape
    return pl.pallas_call(
        combine_kernel,
        in_specs=[whole(), whole()],
        out_specs=whole(),
        out_shape=jax.ShapeDtypeStruct((2 * nx, tokens, rank // 2), BF16),
        compiler_params=pltpu.CompilerParams(vmem_limit_bytes=16 * 1024 * 1024),
    )(parts, picks)


def project_grad_kernel(rows_ref, own_ref, theirs_ref, out_ref):
    core = lax.axis_index("c")
    total = lax.dot_general(
        rows_ref[core], own_ref[...], (((0,), (0,)), ((), ())), preferred_element_type=F32
    )
    total += lax.dot_general(
        rows_ref[1 - core], theirs_ref[...], (((0,), (0,)), ((), ())), preferred_element_type=F32
    )
    out_ref[...] = total.astype(BF16)


def project_grad(rows, own, theirs):
    return pl.pallas_call(
        project_grad_kernel,
        in_specs=[whole(), whole(), whole()],
        out_specs=whole(),
        out_shape=jax.ShapeDtypeStruct((rows.shape[2], own.shape[1]), BF16),
        compiler_params=pltpu.CompilerParams(vmem_limit_bytes=16 * 1024 * 1024),
    )(rows, own, theirs)


def expand_mine_kernel(basis_ref, picks_ref, mine_ref, out_ref, ordered_ref):
    nx, half, _ = mine_ref.shape
    core = lax.axis_index("c")
    for h in range(2):
        pick = picks_ref[core if h == 0 else 1 - core]
        ordered_ref[:, h * half : (h + 1) * half] = jnp.dot(
            basis_ref[...], pick, preferred_element_type=F32
        ).astype(BF16)
    for i in range(nx):
        out_ref[i] = jnp.dot(ordered_ref[:, :half], mine_ref[i], preferred_element_type=F32)


def expand_mine(basis, picks, mine):
    nx, half, cols = mine.shape
    rows = basis.shape[0]
    return pl.pallas_call(
        expand_mine_kernel,
        in_specs=[whole(), whole(), whole()],
        out_specs=[whole(), whole()],
        out_shape=[
            jax.ShapeDtypeStruct((nx, rows, cols), F32),
            jax.ShapeDtypeStruct(basis.shape, BF16),
        ],
        compiler_params=pltpu.CompilerParams(vmem_limit_bytes=24 * 1024 * 1024),
        cost_estimate=pl.CostEstimate(
            flops=2 * rows * half * nx * cols, bytes_accessed=4 * nx * rows * cols, transcendentals=0
        ),
    )(basis, picks, mine)


def expand_kernel(tiles, basis_ref, other_ref, mine_ref, out_ref, done, sems):
    nx, half, cols = other_ref.shape
    size = basis_ref.shape[0] // tiles
    copies = []
    for t in range(tiles):
        rows = pl.ds(t * size, size)
        for i in range(nx):
            acc = mine_ref[i, rows, :] + jnp.dot(
                basis_ref[rows, half:], other_ref[i], preferred_element_type=F32
            )
            done[rows, pl.ds(i * cols, cols)] = acc.astype(BF16)
        copies.append(pltpu.make_async_copy(done.at[rows], out_ref.at[rows], sems.at[t]))
        copies[-1].start()
    for copy in copies:
        copy.wait()


def expand(basis, other, mine, tiles=5):
    nx, half, cols = other.shape
    rows = basis.shape[0]
    return pl.pallas_call(
        functools.partial(expand_kernel, tiles),
        in_specs=[whole(), whole(), whole()],
        out_specs=pl.BlockSpec(memory_space=pl.ANY),
        out_shape=jax.ShapeDtypeStruct((rows, nx * cols), BF16),
        scratch_shapes=[pltpu.VMEM((rows, nx * cols), BF16), pltpu.SemaphoreType.DMA((tiles,))],
        compiler_params=pltpu.CompilerParams(vmem_limit_bytes=24 * 1024 * 1024),
    )(basis, other, mine)


def per_device(ny, nz, nx, inputs, out_grad, basis, moment_first, moment_second):
    rank = basis.shape[1]
    tokens = inputs.shape[0]
    groups = ny * nz
    own, cols = moment_first.shape
    half = rank // 2
    swap = [(0, 1), (1, 0)]

    theirs = lax.ppermute(out_grad, "c", swap)
    picks = rank_order(rank, own)
    partial = project(inputs, basis, picks)
    parts = lax.all_to_all(partial.reshape(nx, tokens // nx, rank), "x", 0, 0)

    sides, theirs = lax.optimization_barrier((combine(parts, picks), theirs))
    rows = lax.all_to_all(sides, ("c", "x"), 0, 0).reshape(2, tokens, half)
    chip = project_grad(rows, out_grad, theirs).reshape(groups, own, cols)
    grad_shard = jnp.sum(lax.all_to_all(chip, ("y", "z"), 0, 0).astype(F32), axis=0)

    new_first = 0.9 * moment_first + 0.1 * grad_shard
    new_second = 0.999 * moment_second + 0.001 * grad_shard * grad_shard
    corrected = new_first / (1.0 - 0.9**STEP)
    scaled = jnp.sqrt(new_second / (1.0 - 0.999**STEP)) + 1e-08
    direction = (corrected / scaled).astype(BF16)

    gathered = spread(direction, ("y", "z"), groups).reshape(half, cols)
    mine = spread(gathered, "x", nx)
    other = lax.ppermute(mine, "c", swap)
    done, ordered = expand_mine(basis, picks, mine)
    return (expand(ordered, other, done), new_first, new_second)


def solution(mesh):
    ny, nz, nx = 8, 8, mesh.devices.shape[1]
    split = Mesh(mesh.devices.reshape(ny, nz, 2, nx), ("y", "z", "c", "x"))
    dp = ("y", "z", "c")

    def body(*args):
        return per_device(ny, nz, nx, *args)

    return jax.shard_map(
        body,
        mesh=split,
        in_specs=(P(dp, "x"), P(dp, "x"), P("x", None), P(dp, "x"), P(dp, "x")),
        out_specs=(P("x", None), P(dp, "x"), P(dp, "x")),
        check_vma=False,
    )
```

time: 110 us -> 108 us (0.982)
  blocking collectives: 62 us -> 83.8 us
  starting transfers between devices: 27 us -> 15.6 us
  waiting for transfers between devices: 9.42 us -> 1.1 us
  local copies, waits for them, and re-layouts: 2.48 us -> 0.37 us
  matrix products: 1.1 us -> 0 us
    all_to_all x0 -> x2, blocking collectives: none -> 21.9 us  [the longest x1 11.4 us: per_device(): rows = lax.all_to_all(sides, ('c', 'x'), 0, 0).reshape(2, tokens, half)]
    all_to_all x2 -> x0, starting transfers between devices: 13 us -> none  [the longest x1 8.12 us: per_device(): rows = lax.all_to_all(sides, ('c', 'x'), 0, 0).reshape(2 * tokens, half)]
    all_to_all x2 -> x0, waiting for transfers between devices: 7.97 us -> none  [the longest x1 7.96 us: per_device(): rows = lax.all_to_all(sides, ('c', 'x'), 0, 0).reshape(2 * tokens, half)]
    unnamed x12 -> x10, local copies, waits for them, and re-layouts: 2.12 us -> 0.02 us
    ppermute x1, starting transfers between devices: 7.42 us -> 8.92 us  [per_device(): theirs = lax.ppermute(out_grad, 'c', swap)]
    dot_general x2 -> x0, matrix products: 1.1 us -> none  [the longest x1 0.58 us: per_device(): jnp.dot(basis, rank_order(rank, own, core), preferred_element_type=F32)]
    pallas_call x3 -> x5, Pallas kernels: 3.43 us -> 2.91 us  [the longest x1 1.54 us: expand_mine(): pl.pallas_call(expand_mine_kernel, in_specs=[whole(), whole(), whole()],...]
  transfers between devices with their start and end apart: 4 -> 2, of which waited for: 2 -> 1; matrix products, arithmetic and copies ran while one was open for 1% -> 0% of each run, Pallas kernels for 2% -> 2%
where the time goes in v4:
time: 108 us; the launch traced here: 107 us
  blocking collectives  83.8 us (78%)
  starting transfers between devices  15.6 us (14%)
  Pallas kernels  5.03 us (5%)
  waiting for transfers between devices  1.1 us (1%)
    all_to_all x2, blocking collectives, spread(): lax.all_to_all(jnp.broadcast_to(block[None], (n,) + block.shape), axes, 0...  35.7 us
    all_to_all x1, blocking collectives, per_device(): lax.all_to_all(chip, ('y', 'z'), 0, 0).astype(F32)  26.2 us
    all_to_all x1, blocking collectives, per_device(): rows = lax.all_to_all(sides, ('c', 'x'), 0, 0).reshape(2, tokens, half)  11.4 us
    all_to_all x1, blocking collectives, per_device(): parts = lax.all_to_all(partial.reshape(nx, tokens // nx, rank), 'x', 0, 0)  10.5 us
    ppermute x1, starting transfers between devices, per_device(): theirs = lax.ppermute(out_grad, 'c', swap)  8.92 us
    ppermute x1, starting transfers between devices, per_device(): other = lax.ppermute(mine, 'c', swap)  6.64 us
  transfers between devices with their start and end apart: 2, of which 1 were waited for; matrix products, arithmetic and copies ran while one was open for 0% of the time, Pallas kernels for 2%

profile of v4, /device:TPU:1, one launch (start us, length us, event | category | flops | bytes accessed | tf_op | source)
XLA Modules:
  0.0 107.4 jit_solution(11149722215038409096)
XLA Ops:
  0.6 0.0 copy-start
  0.6 8.9 %collective-permute-start = (bf16[384,640]{1,0:T(8,128)(2,1)}, bf16[384,640]{1,0:T(8,128)(2,1)S(1)}, u32[]{:S(2)}, u32[]{:S(2)}) collective-permute-start(bf16[384,640]{1,0:T(8,128)(2,1)} %own_ref.1), channel_id=1, source_target_pairs={{0,4},{4,0},{1,5},{5,1},{2,6},{6,2},{3,7},{7,3},{8,12},{12,8},{9,1... | collective-permute-start | bytes 1474568 | tf_op jit(solution)/shard_map/ppermute | solution.py:169
  9.6 0.1 shard_map.76.picks_ref
  9.7 0.5 shard_map.77
  10.2 0.0 copy-start.2
  10.2 10.5 %all_to_all.25.parts_ref = bf16[4,96,512]{2,1,0:T(8,128)(2,1)S(1)} all-to-all(bf16[4,96,512]{2,1,0:T(8,128)(2,1)S(1)} %bitcast.3), channel_id=1, replica_groups=mesh['y'=8,'z'=8,'c'=2,'x'=4] {'x'}, dimensions={0} | all-to-all | bytes 786432 | tf_op jit(solution)/shard_map/all_to_all | solution.py:172
  20.7 0.2 shard_map.78
  20.9 0.0 collective-permute-done.theirs_ref
  20.9 11.4 %all_to_all.26 = bf16[8,96,256]{2,1,0:T(8,128)(2,1)S(1)} all-to-all(bf16[8,96,256]{2,1,0:T(8,128)(2,1)S(1)} %shard_map.78), channel_id=1, replica_groups=mesh['y'=8,'z'=8,'c'=2,'x'=4] {'c','x'}, dimensions={0} | all-to-all | bytes 786432 | tf_op jit(solution)/shard_map/all_to_all | solution.py:175
  32.3 0.6 shard_map.79
  32.9 0.1 reshape.19
  33.0 26.2 %all_to_all.27 = bf16[64,4,640]{2,1,0:T(4,128)(2,1)S(1)} all-to-all(bf16[64,4,640]{2,1,0:T(4,128)(2,1)S(1)} %reshape.19), channel_id=1, replica_groups=mesh['y'=8,'z'=8,'c'=2,'x'=4] {'y','z'}, dimensions={0} | all-to-all | bytes 655360 | tf_op jit(solution)/shard_map/all_to_all | solution.py:177
  59.3 0.2 convert_reduce_fusion
  59.4 0.0 copy-done.3
  59.4 0.6 fusion.1
  60.1 0.1 broadcast_in_dim.6
  60.1 19.1 %all_to_all.28 = bf16[64,4,640]{2,1,0:T(4,128)(2,1)S(1)} all-to-all(bf16[64,4,640]{2,1,0:T(4,128)(2,1)S(1)} %broadcast_in_dim.6), channel_id=1, replica_groups=mesh['y'=8,'z'=8,'c'=2,'x'=4] {'y','z'}, dimensions={0} | all-to-all | bytes 655360 | tf_op jit(solution)/shard_map/all_to_all | solution.py:16
  79.3 0.1 broadcast_in_dim.14
  79.3 0.1 broadcast_in_dim.15
  79.5 16.5 %all_to_all.29.mine_ref = bf16[4,256,640]{2,1,0:T(8,128)(2,1)S(1)} all-to-all(bf16[4,256,640]{2,1,0:T(8,128)(2,1)S(1)} %broadcast_in_dim.15), channel_id=1, replica_groups=mesh['y'=8,'z'=8,'c'=2,'x'=4] {'x'}, dimensions={0} | all-to-all | bytes 2621440 | tf_op jit(solution)/shard_map/all_to_all | solution.py:16
  96.0 6.6 %collective-permute-start.1 = (bf16[4,256,640]{2,1,0:T(8,128)(2,1)S(1)}, bf16[4,256,640]{2,1,0:T(8,128)(2,1)S(1)}, u32[]{:S(2)}, u32[]{:S(2)}) collective-permute-start(bf16[4,256,640]{2,1,0:T(8,128)(2,1)S(1)} %all_to_all.29.mine_ref), channel_id=1, source_target_pairs={{0,4},{4,0},{1,5},{5,1},{2,6},{6,2},{3,7},{7,3},{8,12},{12,8},{9,1... | collective-permute-start | bytes 3932168 | tf_op jit(solution)/shard_map/ppermute | solution.py:187
  102.6 1.5 %shard_map.80 = (f32[4,640,640]{2,1,0:T(8,128)S(1)}, bf16[640,512]{1,0:T(8,128)(2,1)S(1)}) custom-call(bf16[640,512]{1,0:T(8,128)(2,1)S(1)} %copy-done, bf16[2,512,256]{2,1,0:T(8,128)(2,1)S(1)} %shard_map.76.picks_ref, bf16[4,256,640]{2,1,0:T(8,128)(2,1)S(1)} %all_to_all.29.mine_ref), custom_call_target="tpu_custom_call" | custom-call | flops 838860800 | bytes 6553600 | tf_op jit(solution)/shard_map/pallas_call | solution.py:116
  104.2 1.1 %collective-permute-done.1.other_ref = bf16[4,256,640]{2,1,0:T(8,128)(2,1)S(1)} collective-permute-done((bf16[4,256,640]{2,1,0:T(8,128)(2,1)S(1)}, bf16[4,256,640]{2,1,0:T(8,128)(2,1)S(1)}, u32[]{:S(2)}, u32[]{:S(2)}) %collective-permute-start.1) | collective-permute-done | bytes 1310752 | tf_op jit(solution)/shard_map/ppermute | solution.py:187
  105.3 2.1 %shard_map.81 = bf16[640,2560]{1,0:T(8,128)(2,1)} custom-call(bf16[640,512]{1,0:T(8,128)(2,1)S(1)} %get-tuple-element.9.basis_ref, bf16[4,256,640]{2,1,0:T(8,128)(2,1)S(1)} %collective-permute-done.1.other_ref, f32[4,640,640]{2,1,0:T(8,128)S(1)} %get-tuple-element.10.mine_ref), custom_call_target="tpu_custom_call" | custom-call | tf_op jit(solution)/shard_map/pallas_call | solution.py:151
  (7 shorter events, 0.0 us)
Async XLA Ops:
  0.6 9.1 %copy-start = (bf16[640,512]{1,0:T(8,128)(2,1)S(1)}, bf16[640,512]{1,0:T(8,128)(2,1)}, u32[]{:S(2)}) copy-start(bf16[640,512]{1,0:T(8,128)(2,1)} %basis_ref.3) | copy-start | bytes 1966084
  0.6 9.1 %copy-start.1 = (bf16[384,640]{1,0:T(8,128)(2,1)S(1)}, bf16[384,640]{1,0:T(8,128)(2,1)}, u32[]{:S(2)}) copy-start(bf16[384,640]{1,0:T(8,128)(2,1)} %inputs_ref.1) | copy-start | bytes 1474564
  0.6 20.2 %collective-permute-start = (bf16[384,640]{1,0:T(8,128)(2,1)}, bf16[384,640]{1,0:T(8,128)(2,1)S(1)}, u32[]{:S(2)}, u32[]{:S(2)}) collective-permute-start(bf16[384,640]{1,0:T(8,128)(2,1)} %own_ref.1), channel_id=1, source_target_pairs={{0,4},{4,0},{1,5},{5,1},{2,6},{6,2},{3,7},{7,3},{8,12},{12,8},{9,1... | collective-permute-start | bytes 1474568 | tf_op jit(solution)/shard_map/ppermute | solution.py:169
  10.2 22.2 %copy-start.2 = (bf16[384,640]{1,0:T(8,128)(2,1)S(1)}, bf16[384,640]{1,0:T(8,128)(2,1)}, u32[]{:S(2)}) copy-start(bf16[384,640]{1,0:T(8,128)(2,1)} %own_ref.1) | copy-start | bytes 1474564
  32.3 27.1 %copy-start.3 = (f32[4,640]{1,0:T(4,128)S(1)}, f32[4,640]{1,0:T(4,128)}, u32[]{:S(2)}) copy-start(f32[4,640]{1,0:T(4,128)} %param.8) | copy-start | bytes 30724
  32.3 27.1 %copy-start.4 = (f32[4,640]{1,0:T(4,128)S(1)}, f32[4,640]{1,0:T(4,128)}, u32[]{:S(2)}) copy-start(f32[4,640]{1,0:T(4,128)} %param.9) | copy-start | bytes 30724
  96.0 9.3 %collective-permute-start.1 = (bf16[4,256,640]{2,1,0:T(8,128)(2,1)S(1)}, bf16[4,256,640]{2,1,0:T(8,128)(2,1)S(1)}, u32[]{:S(2)}, u32[]{:S(2)}) collective-permute-start(bf16[4,256,640]{2,1,0:T(8,128)(2,1)S(1)} %all_to_all.29.mine_ref), channel_id=1, source_target_pairs={{0,4},{4,0},{1,5},{5,1},{2,6},{6,2},{3,7},{7,3},{8,12},{12,8},{9,1... | collective-permute-start | bytes 3932168 | tf_op jit(solution)/shard_map/ppermute | solution.py:187

commit v5 on v4

--- a/solution.py
+++ b/solution.py
@@ -20,17 +20,22 @@
     return pl.BlockSpec(memory_space=pltpu.VMEM)
 
 
-def order_kernel(own, out_ref):
+def order_kernel(own, ny, nz, out_ref):
     _, rank, half = out_ref.shape
     old = lax.broadcasted_iota(jnp.int32, (rank, half), 0)
     new = lax.broadcasted_iota(jnp.int32, (rank, half), 1)
+    block = new // own
+    pair = block % (nz // 2)
+    y = block // (nz // 2) % ny
+    parity = block // (nz // 2 * ny)
+    first = ((y * nz + pair * 2 + parity) * 2) * own + new % own
     for c in range(2):
-        out_ref[c] = (old == new // own * (2 * own) + c * own + new % own).astype(F32).astype(BF16)
-
-
-def rank_order(rank, own):
-    return pl.pallas_call(
-        functools.partial(order_kernel, own),
+        out_ref[c] = (old == first + c * own).astype(F32).astype(BF16)
+
+
+def rank_order(rank, own, ny, nz):
+    return pl.pallas_call(
+        functools.partial(order_kernel, own, ny, nz),
         in_specs=[],
         out_specs=whole(),
         out_shape=jax.ShapeDtypeStruct((2, rank, rank // 2), BF16),
@@ -98,8 +103,32 @@
     )(rows, own, theirs)
 
 
+def direction_kernel(parts_ref, first_ref, second_ref, grad_ref, out_ref):
+    grad = jnp.sum(parts_ref[...].astype(F32), axis=0)
+    grad_ref[...] = grad
+    new_first = 0.9 * first_ref[...] + 0.1 * grad
+    new_second = 0.999 * second_ref[...] + 0.001 * grad * grad
+    corrected = new_first / (1.0 - 0.9**STEP)
+    scaled = jnp.sqrt(new_second / (1.0 - 0.999**STEP)) + 1e-08
+    out_ref[...] = jnp.broadcast_to((corrected / scaled)[None], out_ref.shape).astype(BF16)
+
+
+def direction_of(parts, first, second, peers):
+    return pl.pallas_call(
+        direction_kernel,
+        in_specs=[whole(), whole(), whole()],
+        out_specs=[whole(), whole()],
+        out_shape=[
+            jax.ShapeDtypeStruct(first.shape, F32),
+            jax.ShapeDtypeStruct((peers,) + parts.shape[1:], BF16),
+        ],
+        compiler_params=pltpu.CompilerParams(vmem_limit_bytes=16 * 1024 * 1024),
+    )(parts, first, second)
+
+
 def expand_mine_kernel(basis_ref, picks_ref, mine_ref, out_ref, ordered_ref):
-    nx, half, _ = mine_ref.shape
+    _, nx, part, _ = mine_ref.shape
+    half = 2 * part
     core = lax.axis_index("c")
     for h in range(2):
         pick = picks_ref[core if h == 0 else 1 - core]
@@ -107,11 +136,12 @@
             basis_ref[...], pick, preferred_element_type=F32
         ).astype(BF16)
     for i in range(nx):
-        out_ref[i] = jnp.dot(ordered_ref[:, :half], mine_ref[i], preferred_element_type=F32)
+        rows = jnp.concatenate([mine_ref[0, i], mine_ref[1, i]], axis=0)
+        out_ref[i] = jnp.dot(ordered_ref[:, :half], rows, preferred_element_type=F32)
 
 
 def expand_mine(basis, picks, mine):
-    nx, half, cols = mine.shape
+    _, nx, part, cols = mine.shape
     rows = basis.shape[0]
     return pl.pallas_call(
         expand_mine_kernel,
@@ -123,20 +153,21 @@
         ],
         compiler_params=pltpu.CompilerParams(vmem_limit_bytes=24 * 1024 * 1024),
         cost_estimate=pl.CostEstimate(
-            flops=2 * rows * half * nx * cols, bytes_accessed=4 * nx * rows * cols, transcendentals=0
+            flops=4 * rows * part * nx * cols, bytes_accessed=4 * nx * rows * cols, transcendentals=0
         ),
     )(basis, picks, mine)
 
 
 def expand_kernel(tiles, basis_ref, other_ref, mine_ref, out_ref, done, sems):
-    nx, half, cols = other_ref.shape
+    _, nx, part, cols = other_ref.shape
     size = basis_ref.shape[0] // tiles
     copies = []
+    others = [jnp.concatenate([other_ref[0, i], other_ref[1, i]], axis=0) for i in range(nx)]
     for t in range(tiles):
         rows = pl.ds(t * size, size)
         for i in range(nx):
             acc = mine_ref[i, rows, :] + jnp.dot(
-                basis_ref[rows, half:], other_ref[i], preferred_element_type=F32
+                basis_ref[rows, 2 * part :], others[i], preferred_element_type=F32
             )
             done[rows, pl.ds(i * cols, cols)] = acc.astype(BF16)
         copies.append(pltpu.make_async_copy(done.at[rows], out_ref.at[rows], sems.at[t]))
@@ -146,7 +177,7 @@
 
 
 def expand(basis, other, mine, tiles=5):
-    nx, half, cols = other.shape
+    _, nx, _, cols = other.shape
     rows = basis.shape[0]
     return pl.pallas_call(
         functools.partial(expand_kernel, tiles),
@@ -167,32 +198,31 @@
     swap = [(0, 1), (1, 0)]
 
     theirs = lax.ppermute(out_grad, "c", swap)
-    picks = rank_order(rank, own)
+    picks = rank_order(rank, own, ny, nz)
     partial = project(inputs, basis, picks)
     parts = lax.all_to_all(partial.reshape(nx, tokens // nx, rank), "x", 0, 0)
 
     sides, theirs = lax.optimization_barrier((combine(parts, picks), theirs))
     rows = lax.all_to_all(sides, ("c", "x"), 0, 0).reshape(2, tokens, half)
     chip = project_grad(rows, out_grad, theirs).reshape(groups, own, cols)
-    grad_shard = jnp.sum(lax.all_to_all(chip, ("y", "z"), 0, 0).astype(F32), axis=0)
-
+    grad_shard, direction = direction_of(
+        lax.all_to_all(chip, ("zl", "y", "zh"), 0, 0), moment_first, moment_second, groups // 2
+    )
+    gathered = lax.all_to_all(direction, ("y", "zh"), 0, 0).reshape(half // 2, cols)
+    mine, grad_shard = lax.optimization_barrier((spread(gathered, ("zl", "x"), 2 * nx), grad_shard))
+    mine = mine.reshape(2, nx, half // 2, cols)
+
+    other = lax.ppermute(mine, "c", swap)
     new_first = 0.9 * moment_first + 0.1 * grad_shard
     new_second = 0.999 * moment_second + 0.001 * grad_shard * grad_shard
-    corrected = new_first / (1.0 - 0.9**STEP)
-    scaled = jnp.sqrt(new_second / (1.0 - 0.999**STEP)) + 1e-08
-    direction = (corrected / scaled).astype(BF16)
-
-    gathered = spread(direction, ("y", "z"), groups).reshape(half, cols)
-    mine = spread(gathered, "x", nx)
-    other = lax.ppermute(mine, "c", swap)
     done, ordered = expand_mine(basis, picks, mine)
     return (expand(ordered, other, done), new_first, new_second)
 
 
 def solution(mesh):
     ny, nz, nx = 8, 8, mesh.devices.shape[1]
-    split = Mesh(mesh.devices.reshape(ny, nz, 2, nx), ("y", "z", "c", "x"))
-    dp = ("y", "z", "c")
+    split = Mesh(mesh.devices.reshape(ny, nz // 2, 2, 2, nx), ("y", "zh", "zl", "c", "x"))
+    dp = ("y", "zh", "zl", "c")
 
     def body(*args):
         return per_device(ny, nz, nx, *args)

time: 108 us -> 105 us (0.972)
  blocking collectives: 83.8 us -> 82.5 us
    all_to_all x2 -> x1, blocking collectives: 35.7 us -> 17.6 us  [spread(): lax.all_to_all(jnp.broadcast_to(block[None], (n,) + block.shape), axes, 0...]
    all_to_all x1 -> x2, blocking collectives: 26.2 us -> 43 us  [the longest x1 24.9 us: per_device(): lax.all_to_all(chip, ('zl', 'y', 'zh'), 0, 0)]
  transfers between devices with their start and end apart: 2 -> 2, of which waited for: 1 -> 1; matrix products, arithmetic and copies ran while one was open for 0% -> 1% of each run, Pallas kernels for 2% -> 2%
where the time goes in v5:
time: 105 us
  blocking collectives  82.5 us (79%)
  starting transfers between devices  15.3 us (15%)
  Pallas kernels  5.24 us (5%)
    all_to_all x1, blocking collectives, per_device(): lax.all_to_all(chip, ('zl', 'y', 'zh'), 0, 0)  24.9 us
    all_to_all x1, blocking collectives, per_device(): lax.all_to_all(direction, ('y', 'zh'), 0, 0).reshape(half // 2, cols)  18.1 us
    all_to_all x1, blocking collectives, spread(): lax.all_to_all(jnp.broadcast_to(block[None], (n,) + block.shape), axes, 0...  17.6 us
    all_to_all x1, blocking collectives, per_device(): rows = lax.all_to_all(sides, ('c', 'x'), 0, 0).reshape(2, tokens, half)  11.4 us
    all_to_all x1, blocking collectives, per_device(): parts = lax.all_to_all(partial.reshape(nx, tokens // nx, rank), 'x', 0, 0)  10.5 us
    ppermute x1, starting transfers between devices, per_device(): theirs = lax.ppermute(out_grad, 'c', swap)  8.92 us
    ppermute x1, starting transfers between devices, per_device(): other = lax.ppermute(mine, 'c', swap)  6.34 us
    pallas_call x1, Pallas kernels, expand(): pl.pallas_call(functools.partial(expand_kernel, tiles), in_specs=[whole()...  2.12 us
  transfers between devices with their start and end apart: 2, of which 1 were waited for; matrix products, arithmetic and copies ran while one was open for 1% of the time, Pallas kernels for 2%

profile of v5, /device:TPU:1, one launch (start us, length us, event | category | flops | bytes accessed | tf_op | source)
XLA Modules:
  0.0 105.1 jit_solution(9622041488546887756)
XLA Ops:
  0.6 0.0 copy-start.1
  0.6 0.0 copy-start
  0.6 8.9 %collective-permute-start = (bf16[384,640]{1,0:T(8,128)(2,1)}, bf16[384,640]{1,0:T(8,128)(2,1)S(1)}, u32[]{:S(2)}, u32[]{:S(2)}) collective-permute-start(bf16[384,640]{1,0:T(8,128)(2,1)} %own_ref.1), channel_id=1, source_target_pairs={{0,4},{4,0},{1,5},{5,1},{2,6},{6,2},{3,7},{7,3},{8,12},{12,8},{9,1... | collective-permute-start | bytes 1474568 | tf_op jit(solution)/shard_map/ppermute | solution.py:200
  9.6 0.1 shard_map.76.picks_ref
  9.7 0.0 copy-done.1
  9.7 0.0 copy-done
  9.7 0.5 shard_map.77
  10.2 0.0 copy-start.2
  10.2 10.5 %all_to_all.25.parts_ref = bf16[4,96,512]{2,1,0:T(8,128)(2,1)S(1)} all-to-all(bf16[4,96,512]{2,1,0:T(8,128)(2,1)S(1)} %bitcast.4), channel_id=1, replica_groups=mesh['y'=8,'zh'=4,'zl'=2,'c'=2,'x'=4] {'x'}, dimensions={0} | all-to-all | bytes 786432 | tf_op jit(solution)/shard_map/all_to_all | solution.py:203
  20.7 0.2 shard_map.78
  20.9 0.0 collective-permute-done.theirs_ref
  20.9 11.4 %all_to_all.26 = bf16[8,96,256]{2,1,0:T(8,128)(2,1)S(1)} all-to-all(bf16[8,96,256]{2,1,0:T(8,128)(2,1)S(1)} %shard_map.78), channel_id=1, replica_groups=mesh['y'=8,'zh'=4,'zl'=2,'c'=2,'x'=4] {'c','x'}, dimensions={0} | all-to-all | bytes 786432 | tf_op jit(solution)/shard_map/all_to_all | solution.py:206
  32.4 0.6 shard_map.79
  32.9 0.1 reshape.21
  33.0 24.9 %all_to_all.27.parts_ref = bf16[64,4,640]{2,1,0:T(4,128)(2,1)S(1)} all-to-all(bf16[64,4,640]{2,1,0:T(4,128)(2,1)S(1)} %reshape.21), channel_id=1, replica_groups=mesh['y'=8,'zh'=4,'zl'=2,'c'=2,'x'=4] {'zl','y','zh'}, dimensions={0} | all-to-all | bytes 655360 | tf_op jit(solution)/shard_map/all_to_all | solution.py:209
  57.9 0.2 shard_map.80
  58.1 18.1 %all_to_all.28 = bf16[32,4,640]{2,1,0:T(4,128)(2,1)S(1)} all-to-all(bf16[32,4,640]{2,1,0:T(4,128)(2,1)S(1)} %get-tuple-element.13), channel_id=1, replica_groups=mesh['y'=8,'zh'=4,'zl'=2,'c'=2,'x'=4] {'y','zh'}, dimensions={0} | all-to-all | bytes 327680 | tf_op jit(solution)/shard_map/all_to_all | solution.py:211
  76.3 0.1 broadcast_in_dim.8
  76.4 17.6 %all_to_all.29 = bf16[8,128,640]{2,1,0:T(8,128)(2,1)S(1)} all-to-all(bf16[8,128,640]{2,1,0:T(8,128)(2,1)S(1)} %broadcast_in_dim.8), channel_id=1, replica_groups=mesh['y'=8,'zh'=4,'zl'=2,'c'=2,'x'=4] {'zl','x'}, dimensions={0} | all-to-all | bytes 2621440 | tf_op jit(solution)/shard_map/all_to_all | solution.py:16
  94.0 6.3 %collective-permute-start.1 = (bf16[2,4,128,640]{3,2,1,0:T(8,128)(2,1)S(1)}, bf16[2,4,128,640]{3,2,1,0:T(8,128)(2,1)S(1)}, u32[]{:S(2)}, u32[]{:S(2)}) collective-permute-start(bf16[2,4,128,640]{3,2,1,0:T(8,128)(2,1)S(1)} %bitcast.5), channel_id=1, source_target_pairs={{0,4},{4,0},{1,5},{5,1},{2,6},{6,2},{3,7},{7,3},{8,12},{12,8},{9,1... | collective-permute-start | bytes 3932168 | tf_op jit(solution)/shard_map/ppermute | solution.py:215
  100.3 1.5 %shard_map.81 = (f32[4,640,640]{2,1,0:T(8,128)S(1)}, bf16[640,512]{1,0:T(8,128)(2,1)S(1)}) custom-call(bf16[640,512]{1,0:T(8,128)(2,1)S(1)} %copy-done, bf16[2,512,256]{2,1,0:T(8,128)(2,1)S(1)} %shard_map.76.picks_ref, bf16[2,4,128,640]{3,2,1,0:T(8,128)(2,1)S(1)} %bitcast.6), custom_call_target="tpu_custom_call" | custom-call | flops 838860800 | bytes 6553600 | tf_op jit(solution)/shard_map/pallas_call | solution.py:146
  101.9 0.6 fusion
  102.5 0.5 collective-permute-done.1.other_ref
  103.0 2.1 %shard_map.82 = bf16[640,2560]{1,0:T(8,128)(2,1)} custom-call(bf16[640,512]{1,0:T(8,128)(2,1)S(1)} %get-tuple-element.16.basis_ref, bf16[2,4,128,640]{3,2,1,0:T(8,128)(2,1)S(1)} %collective-permute-done.1.other_ref, f32[4,640,640]{2,1,0:T(8,128)S(1)} %get-tuple-element.17.mine_ref), custom_call_target="tpu_custom_call" | custom-call | tf_op jit(solution)/shard_map/pallas_call | solution.py:182
  (6 shorter events, 0.1 us)
Async XLA Ops:
  0.6 9.1 %copy-start.1 = (bf16[384,640]{1,0:T(8,128)(2,1)S(1)}, bf16[384,640]{1,0:T(8,128)(2,1)}, u32[]{:S(2)}) copy-start(bf16[384,640]{1,0:T(8,128)(2,1)} %inputs_ref.1) | copy-start | bytes 1474564
  0.6 9.1 %copy-start = (bf16[640,512]{1,0:T(8,128)(2,1)S(1)}, bf16[640,512]{1,0:T(8,128)(2,1)}, u32[]{:S(2)}) copy-start(bf16[640,512]{1,0:T(8,128)(2,1)} %basis_ref.3) | copy-start | bytes 1966084
  0.6 20.3 %collective-permute-start = (bf16[384,640]{1,0:T(8,128)(2,1)}, bf16[384,640]{1,0:T(8,128)(2,1)S(1)}, u32[]{:S(2)}, u32[]{:S(2)}) collective-permute-start(bf16[384,640]{1,0:T(8,128)(2,1)} %own_ref.1), channel_id=1, source_target_pairs={{0,4},{4,0},{1,5},{5,1},{2,6},{6,2},{3,7},{7,3},{8,12},{12,8},{9,1... | collective-permute-start | bytes 1474568 | tf_op jit(solution)/shard_map/ppermute | solution.py:200
  10.2 22.2 %copy-start.2 = (bf16[384,640]{1,0:T(8,128)(2,1)S(1)}, bf16[384,640]{1,0:T(8,128)(2,1)}, u32[]{:S(2)}) copy-start(bf16[384,640]{1,0:T(8,128)(2,1)} %own_ref.1) | copy-start | bytes 1474564
  32.4 25.6 %copy-start.3 = (f32[4,640]{1,0:T(4,128)S(1)}, f32[4,640]{1,0:T(4,128)}, u32[]{:S(2)}) copy-start(f32[4,640]{1,0:T(4,128)} %first_ref.1) | copy-start | bytes 30724
  32.4 25.6 %copy-start.4 = (f32[4,640]{1,0:T(4,128)S(1)}, f32[4,640]{1,0:T(4,128)}, u32[]{:S(2)}) copy-start(f32[4,640]{1,0:T(4,128)} %second_ref.1) | copy-start | bytes 30724
  94.0 9.0 %collective-permute-start.1 = (bf16[2,4,128,640]{3,2,1,0:T(8,128)(2,1)S(1)}, bf16[2,4,128,640]{3,2,1,0:T(8,128)(2,1)S(1)}, u32[]{:S(2)}, u32[]{:S(2)}) collective-permute-start(bf16[2,4,128,640]{3,2,1,0:T(8,128)(2,1)S(1)} %bitcast.5), channel_id=1, source_target_pairs={{0,4},{4,0},{1,5},{5,1},{2,6},{6,2},{3,7},{7,3},{8,12},{12,8},{9,1... | collective-permute-start | bytes 3932168 | tf_op jit(solution)/shard_map/ppermute | solution.py:215

commit v6 on v5

--- a/solution.py
+++ b/solution.py
@@ -68,7 +68,7 @@
     for c in range(2):
         side = jnp.dot(total, picks_ref[c], preferred_element_type=F32).astype(BF16)
         for i in range(nx):
-            out_ref[c * nx + i] = side
+            out_ref[2 * i + c] = side
 
 
 def combine(parts, picks):
@@ -84,11 +84,14 @@
 
 def project_grad_kernel(rows_ref, own_ref, theirs_ref, out_ref):
     core = lax.axis_index("c")
+    nx = rows_ref.shape[0]
+    mine = jnp.concatenate([rows_ref[i, core] for i in range(nx)], axis=0)
+    others = jnp.concatenate([rows_ref[i, 1 - core] for i in range(nx)], axis=0)
     total = lax.dot_general(
-        rows_ref[core], own_ref[...], (((0,), (0,)), ((), ())), preferred_element_type=F32
+        mine, own_ref[...], (((0,), (0,)), ((), ())), preferred_element_type=F32
     )
     total += lax.dot_general(
-        rows_ref[1 - core], theirs_ref[...], (((0,), (0,)), ((), ())), preferred_element_type=F32
+        others, theirs_ref[...], (((0,), (0,)), ((), ())), preferred_element_type=F32
     )
     out_ref[...] = total.astype(BF16)
 
@@ -98,7 +101,7 @@
         project_grad_kernel,
         in_specs=[whole(), whole(), whole()],
         out_specs=whole(),
-        out_shape=jax.ShapeDtypeStruct((rows.shape[2], own.shape[1]), BF16),
+        out_shape=jax.ShapeDtypeStruct((rows.shape[3], own.shape[1]), BF16),
         compiler_params=pltpu.CompilerParams(vmem_limit_bytes=16 * 1024 * 1024),
     )(rows, own, theirs)
 
@@ -127,8 +130,7 @@
 
 
 def expand_mine_kernel(basis_ref, picks_ref, mine_ref, out_ref, ordered_ref):
-    _, nx, part, _ = mine_ref.shape
-    half = 2 * part
+    nx, half, _ = mine_ref.shape
     core = lax.axis_index("c")
     for h in range(2):
         pick = picks_ref[core if h == 0 else 1 - core]
@@ -136,12 +138,11 @@
             basis_ref[...], pick, preferred_element_type=F32
         ).astype(BF16)
     for i in range(nx):
-        rows = jnp.concatenate([mine_ref[0, i], mine_ref[1, i]], axis=0)
-        out_ref[i] = jnp.dot(ordered_ref[:, :half], rows, preferred_element_type=F32)
+        out_ref[i] = jnp.dot(ordered_ref[:, :half], mine_ref[i], preferred_element_type=F32)
 
 
 def expand_mine(basis, picks, mine):
-    _, nx, part, cols = mine.shape
+    nx, half, cols = mine.shape
     rows = basis.shape[0]
     return pl.pallas_call(
         expand_mine_kernel,
@@ -153,21 +154,20 @@
         ],
         compiler_params=pltpu.CompilerParams(vmem_limit_bytes=24 * 1024 * 1024),
         cost_estimate=pl.CostEstimate(
-            flops=4 * rows * part * nx * cols, bytes_accessed=4 * nx * rows * cols, transcendentals=0
+            flops=2 * rows * half * nx * cols, bytes_accessed=4 * nx * rows * cols, transcendentals=0
         ),
     )(basis, picks, mine)
 
 
 def expand_kernel(tiles, basis_ref, other_ref, mine_ref, out_ref, done, sems):
-    _, nx, part, cols = other_ref.shape
+    nx, half, cols = other_ref.shape
     size = basis_ref.shape[0] // tiles
     copies = []
-    others = [jnp.concatenate([other_ref[0, i], other_ref[1, i]], axis=0) for i in range(nx)]
     for t in range(tiles):
         rows = pl.ds(t * size, size)
         for i in range(nx):
             acc = mine_ref[i, rows, :] + jnp.dot(
-                basis_ref[rows, 2 * part :], others[i], preferred_element_type=F32
+                basis_ref[rows, half:], other_ref[i], preferred_element_type=F32
             )
             done[rows, pl.ds(i * cols, cols)] = acc.astype(BF16)
         copies.append(pltpu.make_async_copy(done.at[rows], out_ref.at[rows], sems.at[t]))
@@ -177,7 +177,7 @@
 
 
 def expand(basis, other, mine, tiles=5):
-    _, nx, _, cols = other.shape
+    nx, _, cols = other.shape
     rows = basis.shape[0]
     return pl.pallas_call(
         functools.partial(expand_kernel, tiles),
@@ -203,14 +203,14 @@
     parts = lax.all_to_all(partial.reshape(nx, tokens // nx, rank), "x", 0, 0)
 
     sides, theirs = lax.optimization_barrier((combine(parts, picks), theirs))
-    rows = lax.all_to_all(sides, ("c", "x"), 0, 0).reshape(2, tokens, half)
+    rows = lax.all_to_all(sides, ("x", "c"), 0, 0).reshape(nx, 2, tokens // nx, half)
     chip = project_grad(rows, out_grad, theirs).reshape(groups, own, cols)
     grad_shard, direction = direction_of(
         lax.all_to_all(chip, ("zl", "y", "zh"), 0, 0), moment_first, moment_second, groups // 2
     )
     gathered = lax.all_to_all(direction, ("y", "zh"), 0, 0).reshape(half // 2, cols)
-    mine, grad_shard = lax.optimization_barrier((spread(gathered, ("zl", "x"), 2 * nx), grad_shard))
-    mine = mine.reshape(2, nx, half // 2, cols)
+    mine, grad_shard = lax.optimization_barrier((spread(gathered, ("x", "zl"), 2 * nx), grad_shard))
+    mine = mine.reshape(nx, half, cols)
 
     other = lax.ppermute(mine, "c", swap)
     new_first = 0.9 * moment_first + 0.1 * grad_shard

time: 105 us -> 105 us (level)
  no operation moved by 1% of the time
where the time goes in v6:
time: 105 us
  blocking collectives  82.7 us (79%)
  starting transfers between devices  14.8 us (14%)
  Pallas kernels  5.24 us (5%)
    all_to_all x1, blocking collectives, per_device(): lax.all_to_all(chip, ('zl', 'y', 'zh'), 0, 0)  24.5 us
    all_to_all x1, blocking collectives, per_device(): lax.all_to_all(direction, ('y', 'zh'), 0, 0).reshape(half // 2, cols)  18.3 us
    all_to_all x1, blocking collectives, spread(): lax.all_to_all(jnp.broadcast_to(block[None], (n,) + block.shape), axes, 0...  17.9 us
    all_to_all x1, blocking collectives, per_device(): lax.all_to_all(sides, ('x', 'c'), 0, 0).reshape(nx, 2, tokens // nx, half)  11.6 us
    all_to_all x1, blocking collectives, per_device(): parts = lax.all_to_all(partial.reshape(nx, tokens // nx, rank), 'x', 0, 0)  10.5 us
    ppermute x1, starting transfers between devices, per_device(): theirs = lax.ppermute(out_grad, 'c', swap)  8.92 us
    ppermute x1, starting transfers between devices, per_device(): other = lax.ppermute(mine, 'c', swap)  5.92 us
    pallas_call x1, Pallas kernels, expand(): pl.pallas_call(functools.partial(expand_kernel, tiles), in_specs=[whole()...  2.12 us
  transfers between devices with their start and end apart: 2, of which 1 were waited for; matrix products, arithmetic and copies ran while one was open for 1% of the time, Pallas kernels for 2%

profile of v6, /device:TPU:1, one launch (start us, length us, event | category | flops | bytes accessed | tf_op | source)
XLA Modules:
  0.0 104.9 jit_solution(5643816960943598398)
XLA Ops:
  0.6 0.0 copy-start.1
  0.6 0.0 copy-start
  0.6 8.9 %collective-permute-start = (bf16[384,640]{1,0:T(8,128)(2,1)}, bf16[384,640]{1,0:T(8,128)(2,1)S(1)}, u32[]{:S(2)}, u32[]{:S(2)}) collective-permute-start(bf16[384,640]{1,0:T(8,128)(2,1)} %own_ref.1), channel_id=1, source_target_pairs={{0,4},{4,0},{1,5},{5,1},{2,6},{6,2},{3,7},{7,3},{8,12},{12,8},{9,1... | collective-permute-start | bytes 1474568 | tf_op jit(solution)/shard_map/ppermute | solution.py:200
  9.6 0.1 shard_map.76.picks_ref
  9.7 0.0 copy-done.1
  9.7 0.5 shard_map.77
  10.2 0.0 copy-start.2
  10.2 10.5 %all_to_all.25.parts_ref = bf16[4,96,512]{2,1,0:T(8,128)(2,1)S(1)} all-to-all(bf16[4,96,512]{2,1,0:T(8,128)(2,1)S(1)} %bitcast.4), channel_id=1, replica_groups=mesh['y'=8,'zh'=4,'zl'=2,'c'=2,'x'=4] {'x'}, dimensions={0} | all-to-all | bytes 786432 | tf_op jit(solution)/shard_map/all_to_all | solution.py:203
  20.7 0.2 shard_map.78
  20.9 0.0 collective-permute-done.theirs_ref
  20.9 11.6 %all_to_all.26 = bf16[8,96,256]{2,1,0:T(8,128)(2,1)S(1)} all-to-all(bf16[8,96,256]{2,1,0:T(8,128)(2,1)S(1)} %shard_map.78), channel_id=1, replica_groups=mesh['y'=8,'zh'=4,'zl'=2,'c'=2,'x'=4] {'x','c'}, dimensions={0} | all-to-all | bytes 786432 | tf_op jit(solution)/shard_map/all_to_all | solution.py:206
  32.5 0.6 shard_map.79
  33.1 0.1 reshape.21
  33.1 24.5 %all_to_all.27.parts_ref = bf16[64,4,640]{2,1,0:T(4,128)(2,1)S(1)} all-to-all(bf16[64,4,640]{2,1,0:T(4,128)(2,1)S(1)} %reshape.21), channel_id=1, replica_groups=mesh['y'=8,'zh'=4,'zl'=2,'c'=2,'x'=4] {'zl','y','zh'}, dimensions={0} | all-to-all | bytes 655360 | tf_op jit(solution)/shard_map/all_to_all | solution.py:209
  57.6 0.0 copy-done.3
  57.7 0.2 shard_map.80
  57.9 18.3 %all_to_all.28 = bf16[32,4,640]{2,1,0:T(4,128)(2,1)S(1)} all-to-all(bf16[32,4,640]{2,1,0:T(4,128)(2,1)S(1)} %get-tuple-element.13), channel_id=1, replica_groups=mesh['y'=8,'zh'=4,'zl'=2,'c'=2,'x'=4] {'y','zh'}, dimensions={0} | all-to-all | bytes 327680 | tf_op jit(solution)/shard_map/all_to_all | solution.py:211
  76.2 0.1 broadcast_in_dim.8
  76.3 17.9 %all_to_all.29 = bf16[8,128,640]{2,1,0:T(8,128)(2,1)S(1)} all-to-all(bf16[8,128,640]{2,1,0:T(8,128)(2,1)S(1)} %broadcast_in_dim.8), channel_id=1, replica_groups=mesh['y'=8,'zh'=4,'zl'=2,'c'=2,'x'=4] {'x','zl'}, dimensions={0} | all-to-all | bytes 2621440 | tf_op jit(solution)/shard_map/all_to_all | solution.py:16
  94.2 5.9 %collective-permute-start.1 = (bf16[4,256,640]{2,1,0:T(8,128)(2,1)S(1)}, bf16[4,256,640]{2,1,0:T(8,128)(2,1)S(1)}, u32[]{:S(2)}, u32[]{:S(2)}) collective-permute-start(bf16[4,256,640]{2,1,0:T(8,128)(2,1)S(1)} %bitcast.5), channel_id=1, source_target_pairs={{0,4},{4,0},{1,5},{5,1},{2,6},{6,2},{3,7},{7,3},{8,12},{12,8},{9,1... | collective-permute-start | bytes 3932168 | tf_op jit(solution)/shard_map/ppermute | solution.py:215
  100.2 1.5 %shard_map.81 = (f32[4,640,640]{2,1,0:T(8,128)S(1)}, bf16[640,512]{1,0:T(8,128)(2,1)S(1)}) custom-call(bf16[640,512]{1,0:T(8,128)(2,1)S(1)} %copy-done, bf16[2,512,256]{2,1,0:T(8,128)(2,1)S(1)} %shard_map.76.picks_ref, bf16[4,256,640]{2,1,0:T(8,128)(2,1)S(1)} %bitcast.6), custom_call_target="tpu_custom_call" | custom-call | flops 838860800 | bytes 6553600 | tf_op jit(solution)/shard_map/pallas_call | solution.py:147
  101.7 0.6 fusion
  102.3 0.5 collective-permute-done.1.other_ref
  102.8 2.1 %shard_map.82 = bf16[640,2560]{1,0:T(8,128)(2,1)} custom-call(bf16[640,512]{1,0:T(8,128)(2,1)S(1)} %get-tuple-element.16.basis_ref, bf16[4,256,640]{2,1,0:T(8,128)(2,1)S(1)} %collective-permute-done.1.other_ref, f32[4,640,640]{2,1,0:T(8,128)S(1)} %get-tuple-element.17.mine_ref), custom_call_target="tpu_custom_call" | custom-call | tf_op jit(solution)/shard_map/pallas_call | solution.py:182
  (6 shorter events, 0.1 us)
Async XLA Ops:
  0.6 9.1 %copy-start.1 = (bf16[384,640]{1,0:T(8,128)(2,1)S(1)}, bf16[384,640]{1,0:T(8,128)(2,1)}, u32[]{:S(2)}) copy-start(bf16[384,640]{1,0:T(8,128)(2,1)} %inputs_ref.1) | copy-start | bytes 1474564
  0.6 9.1 %copy-start = (bf16[640,512]{1,0:T(8,128)(2,1)S(1)}, bf16[640,512]{1,0:T(8,128)(2,1)}, u32[]{:S(2)}) copy-start(bf16[640,512]{1,0:T(8,128)(2,1)} %basis_ref.3) | copy-start | bytes 1966084
  0.6 20.3 %collective-permute-start = (bf16[384,640]{1,0:T(8,128)(2,1)}, bf16[384,640]{1,0:T(8,128)(2,1)S(1)}, u32[]{:S(2)}, u32[]{:S(2)}) collective-permute-start(bf16[384,640]{1,0:T(8,128)(2,1)} %own_ref.1), channel_id=1, source_target_pairs={{0,4},{4,0},{1,5},{5,1},{2,6},{6,2},{3,7},{7,3},{8,12},{12,8},{9,1... | collective-permute-start | bytes 1474568 | tf_op jit(solution)/shard_map/ppermute | solution.py:200
  10.2 22.3 %copy-start.2 = (bf16[384,640]{1,0:T(8,128)(2,1)S(1)}, bf16[384,640]{1,0:T(8,128)(2,1)}, u32[]{:S(2)}) copy-start(bf16[384,640]{1,0:T(8,128)(2,1)} %own_ref.1) | copy-start | bytes 1474564
  32.5 25.2 %copy-start.3 = (f32[4,640]{1,0:T(4,128)S(1)}, f32[4,640]{1,0:T(4,128)}, u32[]{:S(2)}) copy-start(f32[4,640]{1,0:T(4,128)} %first_ref.1) | copy-start | bytes 30724
  32.5 25.2 %copy-start.4 = (f32[4,640]{1,0:T(4,128)S(1)}, f32[4,640]{1,0:T(4,128)}, u32[]{:S(2)}) copy-start(f32[4,640]{1,0:T(4,128)} %second_ref.1) | copy-start | bytes 30724
  94.2 8.6 %collective-permute-start.1 = (bf16[4,256,640]{2,1,0:T(8,128)(2,1)S(1)}, bf16[4,256,640]{2,1,0:T(8,128)(2,1)S(1)}, u32[]{:S(2)}, u32[]{:S(2)}) collective-permute-start(bf16[4,256,640]{2,1,0:T(8,128)(2,1)S(1)} %bitcast.5), channel_id=1, source_target_pairs={{0,4},{4,0},{1,5},{5,1},{2,6},{6,2},{3,7},{7,3},{8,12},{12,8},{9,1... | collective-permute-start | bytes 3932168 | tf_op jit(solution)/shard_map/ppermute | solution.py:215

commit v7 on v6

--- a/solution.py
+++ b/solution.py
@@ -45,41 +45,45 @@
 
 
 def project_kernel(inputs_ref, basis_ref, picks_ref, out_ref):
-    del picks_ref
-    out_ref[...] = jnp.dot(inputs_ref[...], basis_ref[...], preferred_element_type=F32).astype(BF16)
-
-
-def project(inputs, basis, picks):
+    size = out_ref.shape[1]
+    part = jnp.dot(inputs_ref[...], basis_ref[...], preferred_element_type=F32).astype(BF16)
+    for c in range(2):
+        side = jnp.dot(part, picks_ref[c], preferred_element_type=F32).astype(BF16)
+        for i in range(out_ref.shape[0] // 2):
+            out_ref[2 * i + c] = side[i * size : (i + 1) * size]
+
+
+def project(inputs, basis, picks, nx):
+    tokens = inputs.shape[0]
     return pl.pallas_call(
         project_kernel,
         in_specs=[whole(), whole(), whole()],
         out_specs=whole(),
-        out_shape=jax.ShapeDtypeStruct((inputs.shape[0], basis.shape[1]), BF16),
+        out_shape=jax.ShapeDtypeStruct((2 * nx, tokens // nx, picks.shape[2]), BF16),
         compiler_params=pltpu.CompilerParams(vmem_limit_bytes=16 * 1024 * 1024),
     )(inputs, basis, picks)
 
 
-def combine_kernel(parts_ref, picks_ref, out_ref):
-    nx = parts_ref.shape[0]
-    total = parts_ref[0].astype(F32)
-    for i in range(1, nx):
-        total += parts_ref[i].astype(F32)
-    total = total.astype(BF16)
+def combine_kernel(parts_ref, out_ref):
+    nx = out_ref.shape[0]
     for c in range(2):
-        side = jnp.dot(total, picks_ref[c], preferred_element_type=F32).astype(BF16)
+        total = parts_ref[c].astype(F32)
+        for i in range(1, nx):
+            total += parts_ref[2 * i + c].astype(F32)
+        total = total.astype(BF16)
         for i in range(nx):
-            out_ref[2 * i + c] = side
-
-
-def combine(parts, picks):
-    nx, tokens, rank = parts.shape
+            out_ref[i, c] = total
+
+
+def combine(parts):
+    both, tokens, half = parts.shape
     return pl.pallas_call(
         combine_kernel,
-        in_specs=[whole(), whole()],
-        out_specs=whole(),
-        out_shape=jax.ShapeDtypeStruct((2 * nx, tokens, rank // 2), BF16),
-        compiler_params=pltpu.CompilerParams(vmem_limit_bytes=16 * 1024 * 1024),
-    )(parts, picks)
+        in_specs=[whole()],
+        out_specs=whole(),
+        out_shape=jax.ShapeDtypeStruct((both // 2, 2, tokens, half), BF16),
+        compiler_params=pltpu.CompilerParams(vmem_limit_bytes=16 * 1024 * 1024),
+    )(parts)
 
 
 def project_grad_kernel(rows_ref, own_ref, theirs_ref, out_ref):
@@ -199,11 +203,9 @@
 
     theirs = lax.ppermute(out_grad, "c", swap)
     picks = rank_order(rank, own, ny, nz)
-    partial = project(inputs, basis, picks)
-    parts = lax.all_to_all(partial.reshape(nx, tokens // nx, rank), "x", 0, 0)
-
-    sides, theirs = lax.optimization_barrier((combine(parts, picks), theirs))
-    rows = lax.all_to_all(sides, ("x", "c"), 0, 0).reshape(nx, 2, tokens // nx, half)
+    parts = lax.all_to_all(project(inputs, basis, picks, nx), ("x", "c"), 0, 0)
+    sums, theirs = lax.optimization_barrier((combine(parts), theirs))
+    rows = lax.all_to_all(sums, "x", 0, 0)
     chip = project_grad(rows, out_grad, theirs).reshape(groups, own, cols)
     grad_shard, direction = direction_of(
         lax.all_to_all(chip, ("zl", "y", "zh"), 0, 0), moment_first, moment_second, groups // 2

time: 105 us -> 103 us (0.981)
  blocking collectives: 82.7 us -> 79.9 us
    all_to_all x2, blocking collectives: 22 us -> 20.2 us  [the longest x1 10.6 us: per_device(): parts = lax.all_to_all(project(inputs, basis, picks, nx), ('x', 'c'), 0, 0)]
where the time goes in v7:
time: 103 us
  blocking collectives  79.9 us (78%)
  starting transfers between devices  15.6 us (15%)
  Pallas kernels  5.32 us (5%)
    all_to_all x1, blocking collectives, per_device(): lax.all_to_all(chip, ('zl', 'y', 'zh'), 0, 0)  24.4 us
    all_to_all x1, blocking collectives, per_device(): lax.all_to_all(direction, ('y', 'zh'), 0, 0).reshape(half // 2, cols)  18 us
    all_to_all x1, blocking collectives, spread(): lax.all_to_all(jnp.broadcast_to(block[None], (n,) + block.shape), axes, 0...  17.4 us
    all_to_all x1, blocking collectives, per_device(): parts = lax.all_to_all(project(inputs, basis, picks, nx), ('x', 'c'), 0, 0)  10.6 us
    all_to_all x1, blocking collectives, per_device(): rows = lax.all_to_all(sums, 'x', 0, 0)  9.58 us
    ppermute x1, starting transfers between devices, per_device(): theirs = lax.ppermute(out_grad, 'c', swap)  8.92 us
    ppermute x1, starting transfers between devices, per_device(): other = lax.ppermute(mine, 'c', swap)  6.65 us
    pallas_call x1, Pallas kernels, expand(): pl.pallas_call(functools.partial(expand_kernel, tiles), in_specs=[whole()...  2.12 us
  transfers between devices with their start and end apart: 2, of which 1 were waited for; matrix products, arithmetic and copies ran while one was open for 1% of the time, Pallas kernels for 2%

profile of v7, /device:TPU:1, one launch (start us, length us, event | category | flops | bytes accessed | tf_op | source)
XLA Modules:
  0.0 102.9 jit_solution(11186416561078989184)
XLA Ops:
  0.6 0.0 copy-start.1
  0.6 0.0 copy-start
  0.6 8.9 %collective-permute-start = (bf16[384,640]{1,0:T(8,128)(2,1)}, bf16[384,640]{1,0:T(8,128)(2,1)S(1)}, u32[]{:S(2)}, u32[]{:S(2)}) collective-permute-start(bf16[384,640]{1,0:T(8,128)(2,1)} %own_ref.1), channel_id=1, source_target_pairs={{0,4},{4,0},{1,5},{5,1},{2,6},{6,2},{3,7},{7,3},{8,12},{12,8},{9,1... | collective-permute-start | bytes 1474568 | tf_op jit(solution)/shard_map/ppermute | solution.py:204
  9.6 0.1 shard_map.76.picks_ref
  9.7 0.0 copy-done.1
  9.7 0.0 copy-done
  9.7 0.7 shard_map.77
  10.4 0.0 copy-start.2
  10.5 10.6 %all_to_all.25.parts_ref = bf16[8,96,256]{2,1,0:T(8,128)(2,1)S(1)} all-to-all(bf16[8,96,256]{2,1,0:T(8,128)(2,1)S(1)} %shard_map.77), channel_id=1, replica_groups=mesh['y'=8,'zh'=4,'zl'=2,'c'=2,'x'=4] {'x','c'}, dimensions={0} | all-to-all | bytes 786432 | tf_op jit(solution)/shard_map/all_to_all | solution.py:206
  21.1 0.1 shard_map.78
  21.1 0.0 collective-permute-done.theirs_ref
  21.1 9.6 %all_to_all.26.rows_ref = bf16[4,2,96,256]{3,2,1,0:T(8,128)(2,1)S(1)} all-to-all(bf16[4,2,96,256]{3,2,1,0:T(8,128)(2,1)S(1)} %shard_map.78), channel_id=1, replica_groups=mesh['y'=8,'zh'=4,'zl'=2,'c'=2,'x'=4] {'x'}, dimensions={0} | all-to-all | bytes 786432 | tf_op jit(solution)/shard_map/all_to_all | solution.py:208
  30.7 0.6 shard_map.79
  31.3 0.1 reshape.13
  31.4 24.4 %all_to_all.27.parts_ref = bf16[64,4,640]{2,1,0:T(4,128)(2,1)S(1)} all-to-all(bf16[64,4,640]{2,1,0:T(4,128)(2,1)S(1)} %reshape.13), channel_id=1, replica_groups=mesh['y'=8,'zh'=4,'zl'=2,'c'=2,'x'=4] {'zl','y','zh'}, dimensions={0} | all-to-all | bytes 655360 | tf_op jit(solution)/shard_map/all_to_all | solution.py:211
  55.8 0.2 shard_map.80
  56.0 18.0 %all_to_all.28 = bf16[32,4,640]{2,1,0:T(4,128)(2,1)S(1)} all-to-all(bf16[32,4,640]{2,1,0:T(4,128)(2,1)S(1)} %get-tuple-element.13), channel_id=1, replica_groups=mesh['y'=8,'zh'=4,'zl'=2,'c'=2,'x'=4] {'y','zh'}, dimensions={0} | all-to-all | bytes 327680 | tf_op jit(solution)/shard_map/all_to_all | solution.py:213
  74.0 0.1 broadcast_in_dim.8
  74.1 17.4 %all_to_all.29 = bf16[8,128,640]{2,1,0:T(8,128)(2,1)S(1)} all-to-all(bf16[8,128,640]{2,1,0:T(8,128)(2,1)S(1)} %broadcast_in_dim.8), channel_id=1, replica_groups=mesh['y'=8,'zh'=4,'zl'=2,'c'=2,'x'=4] {'x','zl'}, dimensions={0} | all-to-all | bytes 2621440 | tf_op jit(solution)/shard_map/all_to_all | solution.py:16
  91.5 6.7 %collective-permute-start.1 = (bf16[4,256,640]{2,1,0:T(8,128)(2,1)S(1)}, bf16[4,256,640]{2,1,0:T(8,128)(2,1)S(1)}, u32[]{:S(2)}, u32[]{:S(2)}) collective-permute-start(bf16[4,256,640]{2,1,0:T(8,128)(2,1)S(1)} %bitcast.1), channel_id=1, source_target_pairs={{0,4},{4,0},{1,5},{5,1},{2,6},{6,2},{3,7},{7,3},{8,12},{12,8},{9,1... | collective-permute-start | bytes 3932168 | tf_op jit(solution)/shard_map/ppermute | solution.py:217
  98.1 1.5 %shard_map.81 = (f32[4,640,640]{2,1,0:T(8,128)S(1)}, bf16[640,512]{1,0:T(8,128)(2,1)S(1)}) custom-call(bf16[640,512]{1,0:T(8,128)(2,1)S(1)} %copy-done, bf16[2,512,256]{2,1,0:T(8,128)(2,1)S(1)} %shard_map.76.picks_ref, bf16[4,256,640]{2,1,0:T(8,128)(2,1)S(1)} %bitcast.2), custom_call_target="tpu_custom_call" | custom-call | flops 838860800 | bytes 6553600 | tf_op jit(solution)/shard_map/pallas_call | solution.py:151
  99.7 0.6 fusion
  100.3 0.5 collective-permute-done.1.other_ref
  100.8 2.1 %shard_map.82 = bf16[640,2560]{1,0:T(8,128)(2,1)} custom-call(bf16[640,512]{1,0:T(8,128)(2,1)S(1)} %get-tuple-element.16.basis_ref, bf16[4,256,640]{2,1,0:T(8,128)(2,1)S(1)} %collective-permute-done.1.other_ref, f32[4,640,640]{2,1,0:T(8,128)S(1)} %get-tuple-element.17.mine_ref), custom_call_target="tpu_custom_call" | custom-call | tf_op jit(solution)/shard_map/pallas_call | solution.py:186
  (6 shorter events, 0.1 us)
Async XLA Ops:
  0.6 9.1 %copy-start.1 = (bf16[384,640]{1,0:T(8,128)(2,1)S(1)}, bf16[384,640]{1,0:T(8,128)(2,1)}, u32[]{:S(2)}) copy-start(bf16[384,640]{1,0:T(8,128)(2,1)} %inputs_ref.1) | copy-start | bytes 1474564
  0.6 9.1 %copy-start = (bf16[640,512]{1,0:T(8,128)(2,1)S(1)}, bf16[640,512]{1,0:T(8,128)(2,1)}, u32[]{:S(2)}) copy-start(bf16[640,512]{1,0:T(8,128)(2,1)} %basis_ref.3) | copy-start | bytes 1966084
  0.6 20.5 %collective-permute-start = (bf16[384,640]{1,0:T(8,128)(2,1)}, bf16[384,640]{1,0:T(8,128)(2,1)S(1)}, u32[]{:S(2)}, u32[]{:S(2)}) collective-permute-start(bf16[384,640]{1,0:T(8,128)(2,1)} %own_ref.1), channel_id=1, source_target_pairs={{0,4},{4,0},{1,5},{5,1},{2,6},{6,2},{3,7},{7,3},{8,12},{12,8},{9,1... | collective-permute-start | bytes 1474568 | tf_op jit(solution)/shard_map/ppermute | solution.py:204
  10.4 20.3 %copy-start.2 = (bf16[384,640]{1,0:T(8,128)(2,1)S(1)}, bf16[384,640]{1,0:T(8,128)(2,1)}, u32[]{:S(2)}) copy-start(bf16[384,640]{1,0:T(8,128)(2,1)} %own_ref.1) | copy-start | bytes 1474564
  30.7 25.1 %copy-start.3 = (f32[4,640]{1,0:T(4,128)S(1)}, f32[4,640]{1,0:T(4,128)}, u32[]{:S(2)}) copy-start(f32[4,640]{1,0:T(4,128)} %first_ref.1) | copy-start | bytes 30724
  30.7 25.1 %copy-start.4 = (f32[4,640]{1,0:T(4,128)S(1)}, f32[4,640]{1,0:T(4,128)}, u32[]{:S(2)}) copy-start(f32[4,640]{1,0:T(4,128)} %second_ref.1) | copy-start | bytes 30724
  91.5 9.3 %collective-permute-start.1 = (bf16[4,256,640]{2,1,0:T(8,128)(2,1)S(1)}, bf16[4,256,640]{2,1,0:T(8,128)(2,1)S(1)}, u32[]{:S(2)}, u32[]{:S(2)}) collective-permute-start(bf16[4,256,640]{2,1,0:T(8,128)(2,1)S(1)} %bitcast.1), channel_id=1, source_target_pairs={{0,4},{4,0},{1,5},{5,1},{2,6},{6,2},{3,7},{7,3},{8,12},{12,8},{9,1... | collective-permute-start | bytes 3932168 | tf_op jit(solution)/shard_map/ppermute | solution.py:217

commit v8 on v7

--- a/solution.py
+++ b/solution.py
@@ -8,8 +8,10 @@
 from jax.sharding import Mesh, PartitionSpec as P
 
 STEP = 10
+MIRRORED = 1
 F32 = jnp.float32
 BF16 = jnp.bfloat16
+PLANE = ("y", "zh", "zl", "c")
 
 
 def spread(block, axes, n):
@@ -29,8 +31,22 @@
     y = block // (nz // 2) % ny
     parity = block // (nz // 2 * ny)
     first = ((y * nz + pair * 2 + parity) * 2) * own + new % own
+    mirrored = (((ny - 1 - y) * nz + (nz // 2 - 1 - pair) * 2 + parity) * 2) * own + new % own
     for c in range(2):
-        out_ref[c] = (old == first + c * own).astype(F32).astype(BF16)
+        start = mirrored if c == MIRRORED else first
+        out_ref[c] = (old == start + c * own).astype(F32).astype(BF16)
+
+
+def plane_groups(ny, nz, parities):
+    pairs = nz // 2
+    groups = []
+    for some in parities:
+        for c in range(2):
+            order = [(p, y, z) for p in some for y in range(ny) for z in range(pairs)]
+            if c == MIRRORED:
+                order = [(p, ny - 1 - y, pairs - 1 - z) for p, y, z in order]
+            groups.append([((y * pairs + z) * 2 + p) * 2 + c for p, y, z in order])
+    return groups
 
 
 def rank_order(rank, own, ny, nz):
@@ -208,9 +224,11 @@
     rows = lax.all_to_all(sums, "x", 0, 0)
     chip = project_grad(rows, out_grad, theirs).reshape(groups, own, cols)
     grad_shard, direction = direction_of(
-        lax.all_to_all(chip, ("zl", "y", "zh"), 0, 0), moment_first, moment_second, groups // 2
-    )
-    gathered = lax.all_to_all(direction, ("y", "zh"), 0, 0).reshape(half // 2, cols)
+        lax.all_to_all(chip, PLANE, 0, 0, axis_index_groups=plane_groups(ny, nz, [(0, 1)])), moment_first, moment_second, groups // 2
+    )
+    gathered = lax.all_to_all(
+        direction, PLANE, 0, 0, axis_index_groups=plane_groups(ny, nz, [(0,), (1,)])
+    ).reshape(half // 2, cols)
     mine, grad_shard = lax.optimization_barrier((spread(gathered, ("x", "zl"), 2 * nx), grad_shard))
     mine = mine.reshape(nx, half, cols)
 

time: 103 us -> 101 us (0.981)
  blocking collectives: 79.9 us -> 73.5 us
  starting transfers between devices: 15.6 us -> 19.8 us
    ppermute x1, starting transfers between devices: 6.65 us -> 10.9 us  [per_device(): other = lax.ppermute(mine, 'c', swap)]
    all_to_all x2, blocking collectives: 42.3 us -> 38.6 us  [the longest x1 23.5 us: per_device(): lax.all_to_all(chip, PLANE, 0, 0, axis_index_groups=plane_groups(ny, nz,...]
    all_to_all x1, blocking collectives: 17.4 us -> 14.7 us  [spread(): lax.all_to_all(jnp.broadcast_to(block[None], (n,) + block.shape), axes, 0...]
where the time goes in v8:
time: 101 us
  blocking collectives  73.5 us (73%)
  starting transfers between devices  19.8 us (20%)
  Pallas kernels  5.33 us (5%)
    all_to_all x1, blocking collectives, per_device(): lax.all_to_all(chip, PLANE, 0, 0, axis_index_groups=plane_groups(ny, nz,...  23.5 us
    all_to_all x1, blocking collectives, per_device(): lax.all_to_all(direction, PLANE, 0, 0, axis_index_groups=plane_groups(ny,...  15.1 us
    all_to_all x1, blocking collectives, spread(): lax.all_to_all(jnp.broadcast_to(block[None], (n,) + block.shape), axes, 0...  14.7 us
    ppermute x1, starting transfers between devices, per_device(): other = lax.ppermute(mine, 'c', swap)  10.9 us
    all_to_all x1, blocking collectives, per_device(): parts = lax.all_to_all(project(inputs, basis, picks, nx), ('x', 'c'), 0, 0)  10.6 us
    all_to_all x1, blocking collectives, per_device(): rows = lax.all_to_all(sums, 'x', 0, 0)  9.58 us
    ppermute x1, starting transfers between devices, per_device(): theirs = lax.ppermute(out_grad, 'c', swap)  8.92 us
    pallas_call x1, Pallas kernels, expand(): pl.pallas_call(functools.partial(expand_kernel, tiles), in_specs=[whole()...  2.12 us
  transfers between devices with their start and end apart: 2, of which 1 were waited for; matrix products, arithmetic and copies ran while one was open for 1% of the time, Pallas kernels for 2%

profile of v8, /device:TPU:1, one launch (start us, length us, event | category | flops | bytes accessed | tf_op | source)
XLA Modules:
  0.0 100.8 jit_solution(17835545038353490853)
XLA Ops:
  0.6 0.0 copy-start.1
  0.6 0.0 copy-start
  0.6 8.9 %collective-permute-start = (bf16[384,640]{1,0:T(8,128)(2,1)}, bf16[384,640]{1,0:T(8,128)(2,1)S(1)}, u32[]{:S(2)}, u32[]{:S(2)}) collective-permute-start(bf16[384,640]{1,0:T(8,128)(2,1)} %own_ref.1), channel_id=1, source_target_pairs={{0,4},{4,0},{1,5},{5,1},{2,6},{6,2},{3,7},{7,3},{8,12},{12,8},{9,1... | collective-permute-start | bytes 1474568 | tf_op jit(solution)/shard_map/ppermute | solution.py:220
  9.6 0.1 shard_map.76.picks_ref
  9.7 0.0 copy-done.1
  9.7 0.7 shard_map.77
  10.4 0.0 copy-start.2
  10.5 10.6 %all_to_all.25.parts_ref = bf16[8,96,256]{2,1,0:T(8,128)(2,1)S(1)} all-to-all(bf16[8,96,256]{2,1,0:T(8,128)(2,1)S(1)} %shard_map.77), channel_id=1, replica_groups=mesh['y'=8,'zh'=4,'zl'=2,'c'=2,'x'=4] {'x','c'}, dimensions={0} | all-to-all | bytes 786432 | tf_op jit(solution)/shard_map/all_to_all | solution.py:222
  21.1 0.1 shard_map.78
  21.1 0.0 collective-permute-done.theirs_ref
  21.1 9.6 %all_to_all.26.rows_ref = bf16[4,2,96,256]{3,2,1,0:T(8,128)(2,1)S(1)} all-to-all(bf16[4,2,96,256]{3,2,1,0:T(8,128)(2,1)S(1)} %shard_map.78), channel_id=1, replica_groups=mesh['y'=8,'zh'=4,'zl'=2,'c'=2,'x'=4] {'x'}, dimensions={0} | all-to-all | bytes 786432 | tf_op jit(solution)/shard_map/all_to_all | solution.py:224
  30.7 0.6 shard_map.79
  31.3 0.1 reshape.13
  31.4 23.5 %all_to_all.27.parts_ref = bf16[64,4,640]{2,1,0:T(4,128)(2,1)S(1)} all-to-all(bf16[64,4,640]{2,1,0:T(4,128)(2,1)S(1)} %reshape.13), channel_id=1, replica_groups={{0,16,32,48,64,80,96,112,128,144,160,176,192,208,224,240,256,272,288,30..., dimensions={0} | all-to-all | bytes 655360 | tf_op jit(solution)/shard_map/all_to_all | solution.py:227
  54.9 0.0 copy-done.3
  54.9 0.2 shard_map.80
  55.1 15.1 %all_to_all.28 = bf16[32,4,640]{2,1,0:T(4,128)(2,1)S(1)} all-to-all(bf16[32,4,640]{2,1,0:T(4,128)(2,1)S(1)} %get-tuple-element.13), channel_id=1, replica_groups={{0,16,32,48,64,80,96,112,128,144,160,176,192,208,224,240,256,272,288,30..., dimensions={0} | all-to-all | bytes 327680 | tf_op jit(solution)/shard_map/all_to_all | solution.py:229
  70.3 0.1 broadcast_in_dim.8
  70.4 14.7 %all_to_all.29 = bf16[8,128,640]{2,1,0:T(8,128)(2,1)S(1)} all-to-all(bf16[8,128,640]{2,1,0:T(8,128)(2,1)S(1)} %broadcast_in_dim.8), channel_id=1, replica_groups=mesh['y'=8,'zh'=4,'zl'=2,'c'=2,'x'=4] {'x','zl'}, dimensions={0} | all-to-all | bytes 2621440 | tf_op jit(solution)/shard_map/all_to_all | solution.py:18
  85.1 10.9 %collective-permute-start.1 = (bf16[4,256,640]{2,1,0:T(8,128)(2,1)S(1)}, bf16[4,256,640]{2,1,0:T(8,128)(2,1)S(1)}, u32[]{:S(2)}, u32[]{:S(2)}) collective-permute-start(bf16[4,256,640]{2,1,0:T(8,128)(2,1)S(1)} %bitcast.1), channel_id=1, source_target_pairs={{0,4},{4,0},{1,5},{5,1},{2,6},{6,2},{3,7},{7,3},{8,12},{12,8},{9,1... | collective-permute-start | bytes 3932168 | tf_op jit(solution)/shard_map/ppermute | solution.py:235
  96.0 1.5 %shard_map.81 = (f32[4,640,640]{2,1,0:T(8,128)S(1)}, bf16[640,512]{1,0:T(8,128)(2,1)S(1)}) custom-call(bf16[640,512]{1,0:T(8,128)(2,1)S(1)} %copy-done, bf16[2,512,256]{2,1,0:T(8,128)(2,1)S(1)} %shard_map.76.picks_ref, bf16[4,256,640]{2,1,0:T(8,128)(2,1)S(1)} %bitcast.2), custom_call_target="tpu_custom_call" | custom-call | flops 838860800 | bytes 6553600 | tf_op jit(solution)/shard_map/pallas_call | solution.py:167
  97.5 0.6 fusion
  98.2 0.5 collective-permute-done.1.other_ref
  98.6 2.1 %shard_map.82 = bf16[640,2560]{1,0:T(8,128)(2,1)} custom-call(bf16[640,512]{1,0:T(8,128)(2,1)S(1)} %get-tuple-element.16.basis_ref, bf16[4,256,640]{2,1,0:T(8,128)(2,1)S(1)} %collective-permute-done.1.other_ref, f32[4,640,640]{2,1,0:T(8,128)S(1)} %get-tuple-element.17.mine_ref), custom_call_target="tpu_custom_call" | custom-call | tf_op jit(solution)/shard_map/pallas_call | solution.py:202
  (6 shorter events, 0.1 us)
Async XLA Ops:
  0.6 9.1 %copy-start.1 = (bf16[384,640]{1,0:T(8,128)(2,1)S(1)}, bf16[384,640]{1,0:T(8,128)(2,1)}, u32[]{:S(2)}) copy-start(bf16[384,640]{1,0:T(8,128)(2,1)} %inputs_ref.1) | copy-start | bytes 1474564
  0.6 9.1 %copy-start = (bf16[640,512]{1,0:T(8,128)(2,1)S(1)}, bf16[640,512]{1,0:T(8,128)(2,1)}, u32[]{:S(2)}) copy-start(bf16[640,512]{1,0:T(8,128)(2,1)} %basis_ref.3) | copy-start | bytes 1966084
  0.6 20.5 %collective-permute-start = (bf16[384,640]{1,0:T(8,128)(2,1)}, bf16[384,640]{1,0:T(8,128)(2,1)S(1)}, u32[]{:S(2)}, u32[]{:S(2)}) collective-permute-start(bf16[384,640]{1,0:T(8,128)(2,1)} %own_ref.1), channel_id=1, source_target_pairs={{0,4},{4,0},{1,5},{5,1},{2,6},{6,2},{3,7},{7,3},{8,12},{12,8},{9,1... | collective-permute-start | bytes 1474568 | tf_op jit(solution)/shard_map/ppermute | solution.py:220
  10.4 20.3 %copy-start.2 = (bf16[384,640]{1,0:T(8,128)(2,1)S(1)}, bf16[384,640]{1,0:T(8,128)(2,1)}, u32[]{:S(2)}) copy-start(bf16[384,640]{1,0:T(8,128)(2,1)} %own_ref.1) | copy-start | bytes 1474564
  30.7 24.2 %copy-start.3 = (f32[4,640]{1,0:T(4,128)S(1)}, f32[4,640]{1,0:T(4,128)}, u32[]{:S(2)}) copy-start(f32[4,640]{1,0:T(4,128)} %first_ref.1) | copy-start | bytes 30724
  30.7 24.2 %copy-start.4 = (f32[4,640]{1,0:T(4,128)S(1)}, f32[4,640]{1,0:T(4,128)}, u32[]{:S(2)}) copy-start(f32[4,640]{1,0:T(4,128)} %second_ref.1) | copy-start | bytes 30724
  85.1 13.5 %collective-permute-start.1 = (bf16[4,256,640]{2,1,0:T(8,128)(2,1)S(1)}, bf16[4,256,640]{2,1,0:T(8,128)(2,1)S(1)}, u32[]{:S(2)}, u32[]{:S(2)}) collective-permute-start(bf16[4,256,640]{2,1,0:T(8,128)(2,1)S(1)} %bitcast.1), channel_id=1, source_target_pairs={{0,4},{4,0},{1,5},{5,1},{2,6},{6,2},{3,7},{7,3},{8,12},{12,8},{9,1... | collective-permute-start | bytes 3932168 | tf_op jit(solution)/shard_map/ppermute | solution.py:235

commit v9 on v8

--- a/solution.py
+++ b/solution.py
@@ -32,9 +32,8 @@
     parity = block // (nz // 2 * ny)
     first = ((y * nz + pair * 2 + parity) * 2) * own + new % own
     mirrored = (((ny - 1 - y) * nz + (nz // 2 - 1 - pair) * 2 + parity) * 2) * own + new % own
-    for c in range(2):
-        start = mirrored if c == MIRRORED else first
-        out_ref[c] = (old == start + c * own).astype(F32).astype(BF16)
+    for n, (start, c) in enumerate([(first, 0), (mirrored, 1), (first, 1)]):
+        out_ref[n] = (old == start + c * own).astype(F32).astype(BF16)
 
 
 def plane_groups(ny, nz, parities):
@@ -54,7 +53,7 @@
         functools.partial(order_kernel, own, ny, nz),
         in_specs=[],
         out_specs=whole(),
-        out_shape=jax.ShapeDtypeStruct((2, rank, rank // 2), BF16),
+        out_shape=jax.ShapeDtypeStruct((3, rank, rank // 2), BF16),
         compiler_params=pltpu.CompilerParams(vmem_limit_bytes=16 * 1024 * 1024),
         cost_estimate=pl.CostEstimate(flops=4 * 10**9, bytes_accessed=8 * 10**6, transcendentals=0),
     )()
@@ -153,7 +152,7 @@
     nx, half, _ = mine_ref.shape
     core = lax.axis_index("c")
     for h in range(2):
-        pick = picks_ref[core if h == 0 else 1 - core]
+        pick = picks_ref[2 * (core if h == 0 else 1 - core)]
         ordered_ref[:, h * half : (h + 1) * half] = jnp.dot(
             basis_ref[...], pick, preferred_element_type=F32
         ).astype(BF16)
@@ -226,9 +225,7 @@
     grad_shard, direction = direction_of(
         lax.all_to_all(chip, PLANE, 0, 0, axis_index_groups=plane_groups(ny, nz, [(0, 1)])), moment_first, moment_second, groups // 2
     )
-    gathered = lax.all_to_all(
-        direction, PLANE, 0, 0, axis_index_groups=plane_groups(ny, nz, [(0,), (1,)])
-    ).reshape(half // 2, cols)
+    gathered = lax.all_to_all(direction, ("y", "zh"), 0, 0).reshape(half // 2, cols)
     mine, grad_shard = lax.optimization_barrier((spread(gathered, ("x", "zl"), 2 * nx), grad_shard))
     mine = mine.reshape(nx, half, cols)
 

time: 101 us -> 104 us (1.030)
  blocking collectives: 73.5 us -> 80.3 us
  starting transfers between devices: 19.8 us -> 15.7 us
    ppermute x1, starting transfers between devices: 10.9 us -> 6.74 us  [per_device(): other = lax.ppermute(mine, 'c', swap)]
    all_to_all x1, blocking collectives: 15.1 us -> 18.7 us  [per_device(): lax.all_to_all(direction, ('y', 'zh'), 0, 0).reshape(half // 2, cols)]
    all_to_all x1, blocking collectives: 14.7 us -> 17.9 us  [spread(): lax.all_to_all(jnp.broadcast_to(block[None], (n,) + block.shape), axes, 0...]
where the time goes in v9:
time: 104 us; the launch traced here: 103 us
  blocking collectives  80.3 us (77%)
  starting transfers between devices  15.7 us (15%)
  Pallas kernels  5.37 us (5%)
    all_to_all x1, blocking collectives, per_device(): lax.all_to_all(chip, PLANE, 0, 0, axis_index_groups=plane_groups(ny, nz,...  23.5 us
    all_to_all x1, blocking collectives, per_device(): lax.all_to_all(direction, ('y', 'zh'), 0, 0).reshape(half // 2, cols)  18.7 us
    all_to_all x1, blocking collectives, spread(): lax.all_to_all(jnp.broadcast_to(block[None], (n,) + block.shape), axes, 0...  17.9 us
    all_to_all x1, blocking collectives, per_device(): parts = lax.all_to_all(project(inputs, basis, picks, nx), ('x', 'c'), 0, 0)  10.6 us
    all_to_all x1, blocking collectives, per_device(): rows = lax.all_to_all(sums, 'x', 0, 0)  9.58 us
    ppermute x1, starting transfers between devices, per_device(): theirs = lax.ppermute(out_grad, 'c', swap)  8.92 us
    ppermute x1, starting transfers between devices, per_device(): other = lax.ppermute(mine, 'c', swap)  6.74 us
    pallas_call x1, Pallas kernels, expand(): pl.pallas_call(functools.partial(expand_kernel, tiles), in_specs=[whole()...  2.12 us
  transfers between devices with their start and end apart: 2, of which 1 were waited for; matrix products, arithmetic and copies ran while one was open for 1% of the time, Pallas kernels for 2%

profile of v9, /device:TPU:1, one launch (start us, length us, event | category | flops | bytes accessed | tf_op | source)
XLA Modules:
  0.0 103.4 jit_solution(9212287642736500536)
XLA Ops:
  0.6 0.0 copy-start.1
  0.6 0.0 copy-start
  0.6 8.9 %collective-permute-start = (bf16[384,640]{1,0:T(8,128)(2,1)}, bf16[384,640]{1,0:T(8,128)(2,1)S(1)}, u32[]{:S(2)}, u32[]{:S(2)}) collective-permute-start(bf16[384,640]{1,0:T(8,128)(2,1)} %own_ref.1), channel_id=1, source_target_pairs={{0,4},{4,0},{1,5},{5,1},{2,6},{6,2},{3,7},{7,3},{8,12},{12,8},{9,1... | collective-permute-start | bytes 1474568 | tf_op jit(solution)/shard_map/ppermute | solution.py:219
  9.6 0.2 shard_map.76.picks_ref
  9.8 0.0 copy-done.1
  9.8 0.0 copy-done
  9.8 0.7 shard_map.77
  10.5 0.0 copy-start.2
  10.5 10.6 %all_to_all.25.parts_ref = bf16[8,96,256]{2,1,0:T(8,128)(2,1)S(1)} all-to-all(bf16[8,96,256]{2,1,0:T(8,128)(2,1)S(1)} %shard_map.77), channel_id=1, replica_groups=mesh['y'=8,'zh'=4,'zl'=2,'c'=2,'x'=4] {'x','c'}, dimensions={0} | all-to-all | bytes 786432 | tf_op jit(solution)/shard_map/all_to_all | solution.py:221
  21.1 0.1 shard_map.78
  21.2 0.0 collective-permute-done.theirs_ref
  21.2 9.6 %all_to_all.26.rows_ref = bf16[4,2,96,256]{3,2,1,0:T(8,128)(2,1)S(1)} all-to-all(bf16[4,2,96,256]{3,2,1,0:T(8,128)(2,1)S(1)} %shard_map.78), channel_id=1, replica_groups=mesh['y'=8,'zh'=4,'zl'=2,'c'=2,'x'=4] {'x'}, dimensions={0} | all-to-all | bytes 786432 | tf_op jit(solution)/shard_map/all_to_all | solution.py:223
  30.8 0.6 shard_map.79
  31.4 0.1 reshape.13
  31.4 23.5 %all_to_all.27.parts_ref = bf16[64,4,640]{2,1,0:T(4,128)(2,1)S(1)} all-to-all(bf16[64,4,640]{2,1,0:T(4,128)(2,1)S(1)} %reshape.13), channel_id=1, replica_groups={{0,16,32,48,64,80,96,112,128,144,160,176,192,208,224,240,256,272,288,30..., dimensions={0} | all-to-all | bytes 655360 | tf_op jit(solution)/shard_map/all_to_all | solution.py:226
  55.0 0.2 shard_map.80
  55.2 18.7 %all_to_all.28 = bf16[32,4,640]{2,1,0:T(4,128)(2,1)S(1)} all-to-all(bf16[32,4,640]{2,1,0:T(4,128)(2,1)S(1)} %get-tuple-element.13), channel_id=1, replica_groups=mesh['y'=8,'zh'=4,'zl'=2,'c'=2,'x'=4] {'y','zh'}, dimensions={0} | all-to-all | bytes 327680 | tf_op jit(solution)/shard_map/all_to_all | solution.py:228
  73.9 0.1 broadcast_in_dim.8
  74.0 17.9 %all_to_all.29 = bf16[8,128,640]{2,1,0:T(8,128)(2,1)S(1)} all-to-all(bf16[8,128,640]{2,1,0:T(8,128)(2,1)S(1)} %broadcast_in_dim.8), channel_id=1, replica_groups=mesh['y'=8,'zh'=4,'zl'=2,'c'=2,'x'=4] {'x','zl'}, dimensions={0} | all-to-all | bytes 2621440 | tf_op jit(solution)/shard_map/all_to_all | solution.py:18
  91.9 6.7 %collective-permute-start.1 = (bf16[4,256,640]{2,1,0:T(8,128)(2,1)S(1)}, bf16[4,256,640]{2,1,0:T(8,128)(2,1)S(1)}, u32[]{:S(2)}, u32[]{:S(2)}) collective-permute-start(bf16[4,256,640]{2,1,0:T(8,128)(2,1)S(1)} %bitcast.1), channel_id=1, source_target_pairs={{0,4},{4,0},{1,5},{5,1},{2,6},{6,2},{3,7},{7,3},{8,12},{12,8},{9,1... | collective-permute-start | bytes 3932168 | tf_op jit(solution)/shard_map/ppermute | solution.py:232
  98.7 1.5 %shard_map.81 = (f32[4,640,640]{2,1,0:T(8,128)S(1)}, bf16[640,512]{1,0:T(8,128)(2,1)S(1)}) custom-call(bf16[640,512]{1,0:T(8,128)(2,1)S(1)} %copy-done, bf16[3,512,256]{2,1,0:T(8,128)(2,1)S(1)} %shard_map.76.picks_ref, bf16[4,256,640]{2,1,0:T(8,128)(2,1)S(1)} %bitcast.2), custom_call_target="tpu_custom_call" | custom-call | flops 838860800 | bytes 6553600 | tf_op jit(solution)/shard_map/pallas_call | solution.py:166
  100.2 0.6 fusion
  100.8 0.5 collective-permute-done.1.other_ref
  101.3 2.1 %shard_map.82 = bf16[640,2560]{1,0:T(8,128)(2,1)} custom-call(bf16[640,512]{1,0:T(8,128)(2,1)S(1)} %get-tuple-element.16.basis_ref, bf16[4,256,640]{2,1,0:T(8,128)(2,1)S(1)} %collective-permute-done.1.other_ref, f32[4,640,640]{2,1,0:T(8,128)S(1)} %get-tuple-element.17.mine_ref), custom_call_target="tpu_custom_call" | custom-call | tf_op jit(solution)/shard_map/pallas_call | solution.py:201
  (6 shorter events, 0.1 us)
Async XLA Ops:
  0.6 9.1 %copy-start.1 = (bf16[384,640]{1,0:T(8,128)(2,1)S(1)}, bf16[384,640]{1,0:T(8,128)(2,1)}, u32[]{:S(2)}) copy-start(bf16[384,640]{1,0:T(8,128)(2,1)} %inputs_ref.1) | copy-start | bytes 1474564
  0.6 9.1 %copy-start = (bf16[640,512]{1,0:T(8,128)(2,1)S(1)}, bf16[640,512]{1,0:T(8,128)(2,1)}, u32[]{:S(2)}) copy-start(bf16[640,512]{1,0:T(8,128)(2,1)} %basis_ref.3) | copy-start | bytes 1966084
  0.6 20.5 %collective-permute-start = (bf16[384,640]{1,0:T(8,128)(2,1)}, bf16[384,640]{1,0:T(8,128)(2,1)S(1)}, u32[]{:S(2)}, u32[]{:S(2)}) collective-permute-start(bf16[384,640]{1,0:T(8,128)(2,1)} %own_ref.1), channel_id=1, source_target_pairs={{0,4},{4,0},{1,5},{5,1},{2,6},{6,2},{3,7},{7,3},{8,12},{12,8},{9,1... | collective-permute-start | bytes 1474568 | tf_op jit(solution)/shard_map/ppermute | solution.py:219
  10.5 20.3 %copy-start.2 = (bf16[384,640]{1,0:T(8,128)(2,1)S(1)}, bf16[384,640]{1,0:T(8,128)(2,1)}, u32[]{:S(2)}) copy-start(bf16[384,640]{1,0:T(8,128)(2,1)} %own_ref.1) | copy-start | bytes 1474564
  30.8 24.2 %copy-start.3 = (f32[4,640]{1,0:T(4,128)S(1)}, f32[4,640]{1,0:T(4,128)}, u32[]{:S(2)}) copy-start(f32[4,640]{1,0:T(4,128)} %first_ref.1) | copy-start | bytes 30724
  30.8 24.2 %copy-start.4 = (f32[4,640]{1,0:T(4,128)S(1)}, f32[4,640]{1,0:T(4,128)}, u32[]{:S(2)}) copy-start(f32[4,640]{1,0:T(4,128)} %second_ref.1) | copy-start | bytes 30724
  91.9 9.4 %collective-permute-start.1 = (bf16[4,256,640]{2,1,0:T(8,128)(2,1)S(1)}, bf16[4,256,640]{2,1,0:T(8,128)(2,1)S(1)}, u32[]{:S(2)}, u32[]{:S(2)}) collective-permute-start(bf16[4,256,640]{2,1,0:T(8,128)(2,1)S(1)} %bitcast.1), channel_id=1, source_target_pairs={{0,4},{4,0},{1,5},{5,1},{2,6},{6,2},{3,7},{7,3},{8,12},{12,8},{9,1... | collective-permute-start | bytes 3932168 | tf_op jit(solution)/shard_map/ppermute | solution.py:232

commit v10 on v8

--- a/solution.py
+++ b/solution.py
@@ -31,7 +31,8 @@
     y = block // (nz // 2) % ny
     parity = block // (nz // 2 * ny)
     first = ((y * nz + pair * 2 + parity) * 2) * own + new % own
-    mirrored = (((ny - 1 - y) * nz + (nz // 2 - 1 - pair) * 2 + parity) * 2) * own + new % own
+    turned_y, turned_pair = block % ny, block // ny % (nz // 2)
+    mirrored = (((ny - 1 - turned_y) * nz + (nz // 2 - 1 - turned_pair) * 2 + parity) * 2) * own + new % own
     for c in range(2):
         start = mirrored if c == MIRRORED else first
         out_ref[c] = (old == start + c * own).astype(F32).astype(BF16)
@@ -44,7 +45,7 @@
         for c in range(2):
             order = [(p, y, z) for p in some for y in range(ny) for z in range(pairs)]
             if c == MIRRORED:
-                order = [(p, ny - 1 - y, pairs - 1 - z) for p, y, z in order]
+                order = [(p, ny - 1 - y, pairs - 1 - z) for p in some for z in range(pairs) for y in range(ny)]
             groups.append([((y * pairs + z) * 2 + p) * 2 + c for p, y, z in order])
     return groups
 

time: 101 us -> 101 us (level)
    all_to_all x1, blocking collectives: 23.5 us -> 22.5 us  [per_device(): lax.all_to_all(chip, PLANE, 0, 0, axis_index_groups=plane_groups(ny, nz,...]
where the time goes in v10:
time: 101 us
  blocking collectives  73.3 us (73%)
  starting transfers between devices  20.1 us (20%)
  Pallas kernels  5.34 us (5%)
    all_to_all x1, blocking collectives, per_device(): lax.all_to_all(chip, PLANE, 0, 0, axis_index_groups=plane_groups(ny, nz,...  22.5 us
    all_to_all x1, blocking collectives, per_device(): lax.all_to_all(direction, PLANE, 0, 0, axis_index_groups=plane_groups(ny,...  15.8 us
    all_to_all x1, blocking collectives, spread(): lax.all_to_all(jnp.broadcast_to(block[None], (n,) + block.shape), axes, 0...  14.8 us
    ppermute x1, starting transfers between devices, per_device(): other = lax.ppermute(mine, 'c', swap)  11.1 us
    all_to_all x1, blocking collectives, per_device(): parts = lax.all_to_all(project(inputs, basis, picks, nx), ('x', 'c'), 0, 0)  10.6 us
    all_to_all x1, blocking collectives, per_device(): rows = lax.all_to_all(sums, 'x', 0, 0)  9.58 us
    ppermute x1, starting transfers between devices, per_device(): theirs = lax.ppermute(out_grad, 'c', swap)  8.92 us
    pallas_call x1, Pallas kernels, expand(): pl.pallas_call(functools.partial(expand_kernel, tiles), in_specs=[whole()...  2.13 us
  transfers between devices with their start and end apart: 2, of which 1 were waited for; matrix products, arithmetic and copies ran while one was open for 1% of the time, Pallas kernels for 2%

profile of v10, /device:TPU:1, one launch (start us, length us, event | category | flops | bytes accessed | tf_op | source)
XLA Modules:
  0.0 100.8 jit_solution(10648131931804934870)
XLA Ops:
  0.6 0.0 copy-start.1
  0.6 0.0 copy-start
  0.6 8.9 %collective-permute-start = (bf16[384,640]{1,0:T(8,128)(2,1)}, bf16[384,640]{1,0:T(8,128)(2,1)S(1)}, u32[]{:S(2)}, u32[]{:S(2)}) collective-permute-start(bf16[384,640]{1,0:T(8,128)(2,1)} %own_ref.1), channel_id=1, source_target_pairs={{0,4},{4,0},{1,5},{5,1},{2,6},{6,2},{3,7},{7,3},{8,12},{12,8},{9,1... | collective-permute-start | bytes 1474568 | tf_op jit(solution)/shard_map/ppermute | solution.py:221
  9.6 0.1 shard_map.76.picks_ref
  9.7 0.0 copy-done.1
  9.7 0.7 shard_map.77
  10.5 0.0 copy-start.2
  10.5 10.6 %all_to_all.25.parts_ref = bf16[8,96,256]{2,1,0:T(8,128)(2,1)S(1)} all-to-all(bf16[8,96,256]{2,1,0:T(8,128)(2,1)S(1)} %shard_map.77), channel_id=1, replica_groups=mesh['y'=8,'zh'=4,'zl'=2,'c'=2,'x'=4] {'x','c'}, dimensions={0} | all-to-all | bytes 786432 | tf_op jit(solution)/shard_map/all_to_all | solution.py:223
  21.1 0.1 shard_map.78
  21.1 0.0 collective-permute-done.theirs_ref
  21.1 9.6 %all_to_all.26.rows_ref = bf16[4,2,96,256]{3,2,1,0:T(8,128)(2,1)S(1)} all-to-all(bf16[4,2,96,256]{3,2,1,0:T(8,128)(2,1)S(1)} %shard_map.78), channel_id=1, replica_groups=mesh['y'=8,'zh'=4,'zl'=2,'c'=2,'x'=4] {'x'}, dimensions={0} | all-to-all | bytes 786432 | tf_op jit(solution)/shard_map/all_to_all | solution.py:225
  30.7 0.0 copy-done.2
  30.7 0.6 shard_map.79
  31.3 0.1 reshape.13
  31.4 22.5 %all_to_all.27.parts_ref = bf16[64,4,640]{2,1,0:T(4,128)(2,1)S(1)} all-to-all(bf16[64,4,640]{2,1,0:T(4,128)(2,1)S(1)} %reshape.13), channel_id=1, replica_groups={{0,16,32,48,64,80,96,112,128,144,160,176,192,208,224,240,256,272,288,30..., dimensions={0} | all-to-all | bytes 655360 | tf_op jit(solution)/shard_map/all_to_all | solution.py:228
  53.9 0.2 shard_map.80
  54.1 15.8 %all_to_all.28 = bf16[32,4,640]{2,1,0:T(4,128)(2,1)S(1)} all-to-all(bf16[32,4,640]{2,1,0:T(4,128)(2,1)S(1)} %get-tuple-element.13), channel_id=1, replica_groups={{0,16,32,48,64,80,96,112,128,144,160,176,192,208,224,240,256,272,288,30..., dimensions={0} | all-to-all | bytes 327680 | tf_op jit(solution)/shard_map/all_to_all | solution.py:230
  69.9 0.1 broadcast_in_dim.8
  70.0 14.8 %all_to_all.29 = bf16[8,128,640]{2,1,0:T(8,128)(2,1)S(1)} all-to-all(bf16[8,128,640]{2,1,0:T(8,128)(2,1)S(1)} %broadcast_in_dim.8), channel_id=1, replica_groups=mesh['y'=8,'zh'=4,'zl'=2,'c'=2,'x'=4] {'x','zl'}, dimensions={0} | all-to-all | bytes 2621440 | tf_op jit(solution)/shard_map/all_to_all | solution.py:18
  84.9 11.1 %collective-permute-start.1 = (bf16[4,256,640]{2,1,0:T(8,128)(2,1)S(1)}, bf16[4,256,640]{2,1,0:T(8,128)(2,1)S(1)}, u32[]{:S(2)}, u32[]{:S(2)}) collective-permute-start(bf16[4,256,640]{2,1,0:T(8,128)(2,1)S(1)} %bitcast.1), channel_id=1, source_target_pairs={{0,4},{4,0},{1,5},{5,1},{2,6},{6,2},{3,7},{7,3},{8,12},{12,8},{9,1... | collective-permute-start | bytes 3932168 | tf_op jit(solution)/shard_map/ppermute | solution.py:236
  96.0 1.5 %shard_map.81 = (f32[4,640,640]{2,1,0:T(8,128)S(1)}, bf16[640,512]{1,0:T(8,128)(2,1)S(1)}) custom-call(bf16[640,512]{1,0:T(8,128)(2,1)S(1)} %copy-done, bf16[2,512,256]{2,1,0:T(8,128)(2,1)S(1)} %shard_map.76.picks_ref, bf16[4,256,640]{2,1,0:T(8,128)(2,1)S(1)} %bitcast.2), custom_call_target="tpu_custom_call" | custom-call | flops 838860800 | bytes 6553600 | tf_op jit(solution)/shard_map/pallas_call | solution.py:168
  97.6 0.6 fusion
  98.2 0.5 collective-permute-done.1.other_ref
  98.7 2.1 %shard_map.82 = bf16[640,2560]{1,0:T(8,128)(2,1)} custom-call(bf16[640,512]{1,0:T(8,128)(2,1)S(1)} %get-tuple-element.16.basis_ref, bf16[4,256,640]{2,1,0:T(8,128)(2,1)S(1)} %collective-permute-done.1.other_ref, f32[4,640,640]{2,1,0:T(8,128)S(1)} %get-tuple-element.17.mine_ref), custom_call_target="tpu_custom_call" | custom-call | tf_op jit(solution)/shard_map/pallas_call | solution.py:203
  (6 shorter events, 0.1 us)
Async XLA Ops:
  0.6 9.1 %copy-start.1 = (bf16[384,640]{1,0:T(8,128)(2,1)S(1)}, bf16[384,640]{1,0:T(8,128)(2,1)}, u32[]{:S(2)}) copy-start(bf16[384,640]{1,0:T(8,128)(2,1)} %inputs_ref.1) | copy-start | bytes 1474564
  0.6 9.1 %copy-start = (bf16[640,512]{1,0:T(8,128)(2,1)S(1)}, bf16[640,512]{1,0:T(8,128)(2,1)}, u32[]{:S(2)}) copy-start(bf16[640,512]{1,0:T(8,128)(2,1)} %basis_ref.3) | copy-start | bytes 1966084
  0.6 20.5 %collective-permute-start = (bf16[384,640]{1,0:T(8,128)(2,1)}, bf16[384,640]{1,0:T(8,128)(2,1)S(1)}, u32[]{:S(2)}, u32[]{:S(2)}) collective-permute-start(bf16[384,640]{1,0:T(8,128)(2,1)} %own_ref.1), channel_id=1, source_target_pairs={{0,4},{4,0},{1,5},{5,1},{2,6},{6,2},{3,7},{7,3},{8,12},{12,8},{9,1... | collective-permute-start | bytes 1474568 | tf_op jit(solution)/shard_map/ppermute | solution.py:221
  10.5 20.3 %copy-start.2 = (bf16[384,640]{1,0:T(8,128)(2,1)S(1)}, bf16[384,640]{1,0:T(8,128)(2,1)}, u32[]{:S(2)}) copy-start(bf16[384,640]{1,0:T(8,128)(2,1)} %own_ref.1) | copy-start | bytes 1474564
  30.7 23.2 %copy-start.3 = (f32[4,640]{1,0:T(4,128)S(1)}, f32[4,640]{1,0:T(4,128)}, u32[]{:S(2)}) copy-start(f32[4,640]{1,0:T(4,128)} %first_ref.1) | copy-start | bytes 30724
  30.7 23.2 %copy-start.4 = (f32[4,640]{1,0:T(4,128)S(1)}, f32[4,640]{1,0:T(4,128)}, u32[]{:S(2)}) copy-start(f32[4,640]{1,0:T(4,128)} %second_ref.1) | copy-start | bytes 30724
  84.9 13.8 %collective-permute-start.1 = (bf16[4,256,640]{2,1,0:T(8,128)(2,1)S(1)}, bf16[4,256,640]{2,1,0:T(8,128)(2,1)S(1)}, u32[]{:S(2)}, u32[]{:S(2)}) collective-permute-start(bf16[4,256,640]{2,1,0:T(8,128)(2,1)S(1)} %bitcast.1), channel_id=1, source_target_pairs={{0,4},{4,0},{1,5},{5,1},{2,6},{6,2},{3,7},{7,3},{8,12},{12,8},{9,1... | collective-permute-start | bytes 3932168 | tf_op jit(solution)/shard_map/ppermute | solution.py:236
